TPU v7x, 256 devices: a whole 4x4x8 slice. The times are simulated.
256 devices in a mesh: intra: 16 (over x, y_lo, core), inter: 16 (over y_hi, z).
Axes of the slice: x: 4, y: 4 (y_hi: 2, y_lo: 2; y = y_hi * 2 + y_lo), z: 8, core: 2. Of those that a mesh axis runs over, the one named last changes fastest.
Arguments:
- hidden_one: bfloat16 [32768, 128], P(('intra', 'inter')), may hold values from -14 to 14
- upstream_one: bfloat16 [32768, 12288], P(('intra', 'inter')), may hold values from -0.0076904297 to 0.0076904297
- hidden_two: bfloat16 [32768, 128], P(('intra', 'inter')), may hold values from -14 to 14
- upstream_two: bfloat16 [32768, 12288], P(('intra', 'inter')), may hold values from -0.0076904297 to 0.0076904297
Outputs:
- grad_one: float32 [128, 12288], P('intra', 'inter')
- grad_two: float32 [128, 12288], P('intra', 'inter')
All inputs are finite; a program needn't handle non-finite values.
Results may differ from a plain program's by a relative error of at most 0.0003.
Values may be sent and summed in bfloat16 or wider, within the bound.
No kernel may reach another device: no remote copies, remote signals or barrier semaphores. Data moves between devices by JAX's collectives and lax.ppermute only.
A program may use at most 128 MiB of HBM per device.

v0:
```python
import functools

import jax
import jax.numpy as jnp
from jax import lax
from jax.experimental import pallas as pl
from jax.experimental.pallas import tpu as pltpu
from jax.sharding import PartitionSpec as P

BLOCK = 128
SHARE = 8
LOWEST = 2.0**-34
X, Y, CORES = 4, 2, 2
OWNERS = 16
STEPS = OWNERS // 2
LAYER = 6
FIRST = 4
ROOM = (50, 46, 46)
SMALL = pl.CostEstimate(flops=1, bytes_accessed=1, transcendentals=0)
PARAMS = pltpu.CompilerParams(vmem_limit_bytes=32 * 2**20)


def node_pairs(move):
    pairs = []
    for x in range(X):
        for y in range(Y):
            for core in range(CORES):
                to_x, to_y, to_core = move(x, y, core)
                pairs.append(((x * Y + y) * CORES + core, (to_x % X * Y + to_y) * CORES + to_core))
    return pairs


TO_CORE = node_pairs(lambda x, y, core: (x, y, 1 - core))
TO_Y = node_pairs(lambda x, y, core: (x, 1 - y, core))
TO_FIRST = node_pairs(lambda x, y, core: (x + 1 - 2 * (x % 2), y, core))
TO_SECOND = node_pairs(lambda x, y, core: (x - 1 + 2 * (x % 2), y, core))


def send(array, pairs):
    return lax.ppermute(array, "intra", pairs)


def round_to_step(values):
    largest = jnp.maximum(jnp.max(jnp.abs(values), axis=-1, keepdims=True), LOWEST)
    gap = largest - largest * (1.0 - 2.0**-24)
    step = gap * 2.0**18
    half = gap * 2.0**17
    shift = gap * (1.5 * 2.0**41)
    nearest = (values + shift) - shift
    return nearest + jnp.where(values - nearest >= half, step, 0.0)


def ordered(hidden, me, along_y_first):
    rows = hidden.shape[1]
    place = lax.broadcasted_iota(jnp.int32, (rows, rows), 0)
    row = lax.broadcasted_iota(jnp.int32, (rows, rows), 1)
    core = place // 64
    if along_y_first:
        y, x = place // 32 % 2, place // 8 % 4
    else:
        x, y = place // 16 % 4, place // 8 % 2
    own_x = me // 4
    x = (own_x + x * (1 - 2 * (own_x % 2)) + X) % X
    y = (y + me // 2) % Y
    core = (core + me) % CORES
    source = ((x * Y + y) * CORES + core) * SHARE + place % SHARE
    chosen = jnp.where(row == source, 1.0, 0.0).astype(jnp.bfloat16)
    return lax.dot_general(
        chosen, hidden, (((1,), (1,)), ((), ())), preferred_element_type=jnp.float32
    ).astype(jnp.bfloat16)


def gradient_kernel(share, along_y_first, waits, me_ref, hidden_ref, upstream_ref, *refs):
    if waits:
        refs = refs[waits:]
    keep_ref, send_ref, place, arrived = refs
    rows = 2 * SHARE * len(share)
    width = len(share) * BLOCK

    def copies(step):
        found = []
        for owner in range(2):
            start = (step * 2 + owner) * LAYER * BLOCK + share[0] * BLOCK
            source = upstream_ref.at[:, pl.ds(pl.multiple_of(start, BLOCK), width)]
            found.append(pltpu.make_async_copy(source, place.at[step, owner], arrived.at[step, owner]))
        return found

    for step in range(STEPS):
        for copy in copies(step):
            copy.start()
    left = ordered(hidden_ref[...], me_ref[0], along_y_first)

    def one_step(step, carry):
        for copy in copies(step):
            copy.wait()
        blocks = [(owner, block) for owner in range(2) for block in range(len(share))]
        for pair in range(len(share)):
            both = []
            for owner, block in blocks[2 * pair : 2 * pair + 2]:
                upstream = place[step, owner, :, block * BLOCK : (block + 1) * BLOCK]
                grad = jnp.dot(left, upstream, preferred_element_type=jnp.float32)
                both.append(round_to_step(grad).reshape(16, SHARE, BLOCK))
            both = jnp.concatenate(both, axis=1).astype(jnp.bfloat16)
            at = pl.ds(pl.multiple_of(step * rows + pair * 2 * SHARE, 2 * SHARE), 2 * SHARE)
            keep_ref[:, at, :] = both[:8]
            send_ref[:, at, :] = both[8:]
        return carry

    lax.fori_loop(0, STEPS, one_step, 0)


def gradients(me, hidden, upstream, share, along_y_first, room, after=()):
    tokens = upstream.shape[0]
    out = jax.ShapeDtypeStruct((8, OWNERS * len(share) * SHARE, BLOCK), jnp.bfloat16)
    return pl.pallas_call(
        functools.partial(gradient_kernel, share, along_y_first, len(after)),
        in_specs=[
            pl.BlockSpec(memory_space=pltpu.SMEM),
            pl.BlockSpec(memory_space=pltpu.VMEM),
            pl.BlockSpec(memory_space=pltpu.HBM),
        ]
        + [pl.BlockSpec(memory_space=pl.ANY)] * len(after),
        out_specs=[pl.BlockSpec(memory_space=pltpu.VMEM)] * 2,
        out_shape=[out, out],
        scratch_shapes=[
            pltpu.VMEM((STEPS, 2, tokens, len(share) * BLOCK), jnp.bfloat16),
            pltpu.SemaphoreType.DMA((STEPS, 2)),
        ],
        compiler_params=pltpu.CompilerParams(vmem_limit_bytes=room * 2**20),
        cost_estimate=SMALL,
    )(me, hidden, upstream, *after)


def tiled_call(kernel, steps, ins, outs, after=()):
    if after:
        inner = kernel

        def kernel(*refs):
            inner(*refs[: len(ins)], *refs[len(ins) + len(after) :])

    def spec(shape):
        tile = shape[-2] // steps
        lead = len(shape) - 2
        return pl.BlockSpec(shape[:-2] + (tile, BLOCK), lambda c: (0,) * lead + (c, 0))

    shapes = [jax.ShapeDtypeStruct(tuple(lead) + (rows, BLOCK), dtype) for lead, rows, dtype in outs]
    return pl.pallas_call(
        kernel,
        grid=(steps,),
        in_specs=[spec(a.shape) for a in ins] + [pl.BlockSpec(memory_space=pl.ANY)] * len(after),
        out_specs=[spec(s.shape) for s in shapes],
        out_shape=shapes,
        compiler_params=PARAMS,
        cost_estimate=SMALL,
    )(*ins, *after)


def up(ref, *index):
    return ref[index].astype(jnp.float32) if index else ref[...].astype(jnp.float32)


def pair_kernel(keep_ref, got_ref, stay_ref, go_ref):
    for part in range(4):
        stay_ref[part] = up(keep_ref, part) + up(got_ref, part)
        go_ref[part] = up(keep_ref, part + 4) + up(got_ref, part + 4)


def add_kernel(keep_ref, got_ref, own_ref, first_ref, second_ref, first_later_ref, second_later_ref):
    def total(x, half):
        return up(keep_ref, x, half) + up(got_ref, x, half)

    own_ref[0], own_ref[1] = total(0, 0), total(0, 1)
    first_ref[0], first_ref[1] = total(2, 0), total(1, 0)
    second_ref[0], second_ref[1] = total(2, 1), total(3, 1)
    first_later_ref[...] = total(1, 1)
    second_later_ref[...] = total(3, 0)


def fold_kernel(first_ref, second_ref, from_first_ref, from_second_ref, to_first_ref, to_second_ref):
    to_first_ref[...] = first_ref[...] + from_second_ref[0]
    to_second_ref[...] = second_ref[...] + from_first_ref[0]


def halves(own_ref, from_first_ref, from_second_ref, later_first_ref, later_second_ref):
    first = own_ref[0] + from_first_ref[1] + later_second_ref[...]
    second = own_ref[1] + from_second_ref[1] + later_first_ref[...]
    return first, second


def node_pairs_kernel(own_ref, from_first_ref, from_second_ref, later_first_ref, later_second_ref, stay_ref, go_ref):
    stay_ref[...], go_ref[...] = halves(own_ref, from_first_ref, from_second_ref, later_first_ref, later_second_ref)


def nodes_kernel(*refs):
    out_ref = refs[-1]
    parts = []
    for share in (refs[:5], refs[5:10]):
        parts.append(jnp.concatenate([round_to_step(half).astype(jnp.bfloat16) for half in halves(*share)], axis=0))
    stay_ref, got_ref = refs[10:12]
    parts.append(round_to_step(stay_ref[...] + got_ref[...]).astype(jnp.bfloat16))
    at = 0
    for part in parts:
        rows = part.shape[0] // OWNERS
        for owner in range(OWNERS):
            out_ref[owner, at : at + rows] = part[owner * rows : (owner + 1) * rows]
        at += rows


def final_kernel(pieces_ref, one_ref, two_ref):
    total = up(pieces_ref, 0)
    for source in range(1, OWNERS):
        total = total + up(pieces_ref, source)
    for block in range(LAYER):
        columns = slice(block * BLOCK, (block + 1) * BLOCK)
        one_ref[:, columns] = total[block * SHARE : (block + 1) * SHARE]
        two_ref[:, columns] = total[(LAYER + block) * SHARE : (LAYER + block + 1) * SHARE]


def start_x(keep, got, after=()):
    rows = keep.shape[2]
    f32 = jnp.float32
    own, first, second, first_later, second_later = tiled_call(
        add_kernel, 4, (keep, got), [((2,), rows, f32)] * 3 + [((), rows, f32)] * 2, after
    )
    return own, first_later, second_later, send(first, TO_FIRST), send(second, TO_SECOND)


def end_x(own, first_later, second_later, from_first, from_second, after=()):
    rows = own.shape[1]
    first, second = tiled_call(
        fold_kernel, 1, (first_later, second_later, from_first, from_second), [((), rows, jnp.float32)] * 2, after
    )
    return (own, from_first, from_second, send(first, TO_FIRST), send(second, TO_SECOND)), (first, second)


def body(hidden_one, upstream_one, hidden_two, upstream_two):
    f32, bf16 = jnp.float32, jnp.bfloat16
    me = lax.axis_index("intra").astype(jnp.int32).reshape(1)

    def pair(keep, got, after=()):
        return tiled_call(pair_kernel, 4, (keep, got), [((4,), keep.shape[1], f32)] * 2, after)

    def halved(array, parts):
        rows = array.size // BLOCK // parts // 2
        return array.reshape(parts, 2, rows, BLOCK)

    keep_b, go_b = gradients(me, hidden_two, upstream_two, tuple(range(LAYER)), False, ROOM[0])
    core_b = send(go_b, TO_CORE)
    keep_a, go_a = gradients(me, hidden_one, upstream_one, tuple(range(FIRST)), True, ROOM[1])
    core_a = send(go_a, TO_CORE)
    b = start_x(halved(keep_b, 4), halved(core_b, 4))
    stay_a, go_a = pair(keep_a, core_a, (b[0],))
    y_a = send(go_a, TO_Y)
    keep_c, go_c = gradients(me, hidden_one, upstream_one, tuple(range(FIRST, LAYER)), True, ROOM[2], (stay_a,))
    core_c = send(go_c, TO_CORE)
    stay_c, go_c = pair(keep_c, core_c)
    y_c = send(go_c, TO_Y)

    b, sent_b = end_x(*b, (go_c,))
    a = start_x(halved(stay_a, 4), halved(y_a, 4), sent_b)
    stay_b, go_b = tiled_call(node_pairs_kernel, 2, b, [((), b[0].shape[1], f32)] * 2, (a[0],))
    y_b = send(go_b, TO_Y)
    c = start_x(halved(stay_c, 4), halved(y_c, 4), (go_b,))
    a, sent_a = end_x(*a, (c[0],))
    c, _ = end_x(*c, sent_a)

    node = pl.pallas_call(
        nodes_kernel,
        out_shape=jax.ShapeDtypeStruct((OWNERS, 2 * LAYER * SHARE, BLOCK), bf16),
        compiler_params=PARAMS,
        cost_estimate=SMALL,
    )(*a, *c, stay_b, y_b)
    pieces = lax.all_to_all(node, "inter", split_axis=0, concat_axis=0, tiled=True)
    out = jax.ShapeDtypeStruct((SHARE, LAYER * BLOCK), f32)
    return pl.pallas_call(final_kernel, out_shape=(out, out))(pieces)


def solution(mesh):
    return jax.shard_map(
        body,
        mesh=mesh,
        in_specs=(
            P(("intra", "inter"), None),
            P(("intra", "inter"), None),
            P(("intra", "inter"), None),
            P(("intra", "inter"), None),
        ),
        out_specs=(P("intra", "inter"), P("intra", "inter")),
        check_vma=False,
    )
```

profile of v0, /device:TPU:32, one launch (start us, length us, event | category | flops | bytes accessed | tf_op | source)
XLA Modules:
  0.0 92.5 jit_solution(11000329354317974174)
XLA Ops:
  0.6 0.7 copy-done.2
  1.4 5.9 %shard_map.60 = (bf16[8,768,128]{2,1,0:T(8,128)(2,1)S(1)}, bf16[8,768,128]{2,1,0:T(8,128)(2,1)S(1)}) custom-call(s32[1]{0:T(128)} %bitcast.me_ref, bf16[128,128]{1,0:T(8,128)(2,1)S(1)} %copy-done.2, bf16[128,12288]{1,0:T(8,128)(2,1)} %upstream_ref.4), custom_call_target="tpu_custom_call" | custom-call | flops 1 | bytes 1 | tf_op jit(solution)/shard_map/pallas_call | solution.py:115
  7.3 0.1 collective-permute-start.1
  7.4 4.3 %shard_map.59 = (bf16[8,512,128]{2,1,0:T(8,128)(2,1)S(1)}, bf16[8,512,128]{2,1,0:T(8,128)(2,1)S(1)}) custom-call(s32[1]{0:T(128)} %bitcast.me_ref, bf16[128,128]{1,0:T(8,128)(2,1)S(1)} %copy-done.1, bf16[128,12288]{1,0:T(8,128)(2,1)S(1)} %copy-done), custom_call_target="tpu_custom_call" | custom-call | flops 1 | bytes 1 | tf_op jit(solution)/shard_map/pallas_call | solution.py:115
  11.7 0.6 collective-permute-start
  12.3 0.8 shard_map.61
  13.1 1.6 %collective-permute-start.3 = (f32[2,768,128]{2,1,0:T(8,128)S(1)}, f32[2,768,128]{2,1,0:T(8,128)S(1)}, u32[]{:S(2)}, u32[]{:S(2)}) collective-permute-start(f32[2,768,128]{2,1,0:T(8,128)S(1)} %get-tuple-element.44), channel_id=1, source_target_pairs={{0,64},{16,80},{32,96},{48,112},{64,0},{80,16},{96,32},{112,48},{1... | collective-permute-start | bytes 2359304 | tf_op jit(solution)/shard_map/ppermute | solution.py:40
  14.7 2.1 %collective-permute-start.4 = (f32[2,768,128]{2,1,0:T(8,128)S(1)}, f32[2,768,128]{2,1,0:T(8,128)S(1)}, u32[]{:S(2)}, u32[]{:S(2)}) collective-permute-start(f32[2,768,128]{2,1,0:T(8,128)S(1)} %get-tuple-element.45), channel_id=1, source_target_pairs={{0,192},{16,208},{32,224},{48,240},{64,128},{80,144},{96,160},{112... | collective-permute-start | bytes 2359304 | tf_op jit(solution)/shard_map/ppermute | solution.py:40
  16.8 0.6 shard_map.62
  17.3 1.7 %collective-permute-start.2 = (f32[4,512,128]{2,1,0:T(8,128)S(1)}, f32[4,512,128]{2,1,0:T(8,128)S(1)}, u32[]{:S(2)}, u32[]{:S(2)}) collective-permute-start(f32[4,512,128]{2,1,0:T(8,128)S(1)} %get-tuple-element.41), channel_id=1, source_target_pairs={{0,32},{16,48},{32,0},{48,16},{64,96},{80,112},{96,64},{112,80},{1... | collective-permute-start | bytes 3145736 | tf_op jit(solution)/shard_map/ppermute | solution.py:40
  19.0 3.2 %shard_map.63 = (bf16[8,256,128]{2,1,0:T(8,128)(2,1)S(1)}, bf16[8,256,128]{2,1,0:T(8,128)(2,1)S(1)}) custom-call(s32[1]{0:T(128)} %bitcast.me_ref, bf16[128,128]{1,0:T(8,128)(2,1)S(1)} %copy-done.1, bf16[128,12288]{1,0:T(8,128)(2,1)S(1)} %copy-done, f32[4,512,128]{2,1,0:T(8,128)S(1)} %get-tuple-element.40.refs_0_), custom_call_target="tpu_custom_call" | custom-call | flops 1 | bytes 1 | tf_op jit(solution)/shard_map/pallas_call | solution.py:115
  22.2 0.1 collective-permute-start.5
  22.3 1.9 %collective-permute-done.5.got_ref = bf16[8,256,128]{2,1,0:T(8,128)(2,1)S(1)} collective-permute-done((bf16[8,256,128]{2,1,0:T(8,128)(2,1)S(1)}, bf16[8,256,128]{2,1,0:T(8,128)(2,1)S(1)}, u32[]{:S(2)}, u32[]{:S(2)}) %collective-permute-start.5) | collective-permute-done | bytes 524320 | tf_op jit(solution)/shard_map/ppermute | solution.py:40
  24.2 0.3 shard_map.64
  24.6 8.1 %collective-permute-done.3.refs_2_.refs_1_ = f32[2,768,128]{2,1,0:T(8,128)S(1)} collective-permute-done((f32[2,768,128]{2,1,0:T(8,128)S(1)}, f32[2,768,128]{2,1,0:T(8,128)S(1)}, u32[]{:S(2)}, u32[]{:S(2)}) %collective-permute-start.3) | collective-permute-done | bytes 786464 | tf_op jit(solution)/shard_map/ppermute | solution.py:40
  32.7 2.4 %collective-permute-done.4.refs_3_.refs_2_ = f32[2,768,128]{2,1,0:T(8,128)S(1)} collective-permute-done((f32[2,768,128]{2,1,0:T(8,128)S(1)}, f32[2,768,128]{2,1,0:T(8,128)S(1)}, u32[]{:S(2)}, u32[]{:S(2)}) %collective-permute-start.4) | collective-permute-done | bytes 786464 | tf_op jit(solution)/shard_map/ppermute | solution.py:40
  35.1 0.1 shard_map.65
  35.2 2.2 %collective-permute-start.10 = (f32[768,128]{1,0:T(8,128)S(1)}, f32[768,128]{1,0:T(8,128)S(1)}, u32[]{:S(2)}, u32[]{:S(2)}) collective-permute-start(f32[768,128]{1,0:T(8,128)S(1)} %get-tuple-element.50.refs_3_), channel_id=1, source_target_pairs={{0,192},{16,208},{32,224},{48,240},{64,128},{80,144},{96,160},{112... | collective-permute-start | bytes 1179656 | tf_op jit(solution)/shard_map/ppermute | solution.py:40
  37.3 0.0 collective-permute-start.9
  37.3 1.6 %collective-permute-start.8 = (f32[4,256,128]{2,1,0:T(8,128)S(1)}, f32[4,256,128]{2,1,0:T(8,128)S(1)}, u32[]{:S(2)}, u32[]{:S(2)}) collective-permute-start(f32[4,256,128]{2,1,0:T(8,128)S(1)} %get-tuple-element.48.refs_4_), channel_id=1, source_target_pairs={{0,32},{16,48},{32,0},{48,16},{64,96},{80,112},{96,64},{112,80},{1... | collective-permute-start | bytes 1572872 | tf_op jit(solution)/shard_map/ppermute | solution.py:40
  38.9 4.6 %collective-permute-done.2 = f32[4,512,128]{2,1,0:T(8,128)S(1)} collective-permute-done((f32[4,512,128]{2,1,0:T(8,128)S(1)}, f32[4,512,128]{2,1,0:T(8,128)S(1)}, u32[]{:S(2)}, u32[]{:S(2)}) %collective-permute-start.2) | collective-permute-done | bytes 1048608 | tf_op jit(solution)/shard_map/ppermute | solution.py:40
  43.5 0.4 shard_map.66
  43.9 0.7 collective-permute-start.6
  44.6 0.7 collective-permute-start.7
  45.3 2.2 %collective-permute-done.10.refs_4_ = f32[768,128]{1,0:T(8,128)S(1)} collective-permute-done((f32[768,128]{1,0:T(8,128)S(1)}, f32[768,128]{1,0:T(8,128)S(1)}, u32[]{:S(2)}, u32[]{:S(2)}) %collective-permute-start.10) | collective-permute-done | bytes 393248 | tf_op jit(solution)/shard_map/ppermute | solution.py:40
  47.5 1.9 %collective-permute-done.9.refs_3_ = f32[768,128]{1,0:T(8,128)S(1)} collective-permute-done((f32[768,128]{1,0:T(8,128)S(1)}, f32[768,128]{1,0:T(8,128)S(1)}, u32[]{:S(2)}, u32[]{:S(2)}) %collective-permute-start.9) | collective-permute-done | bytes 393248 | tf_op jit(solution)/shard_map/ppermute | solution.py:40
  49.4 0.3 shard_map.67
  49.7 1.7 %collective-permute-start.17 = (f32[768,128]{1,0:T(8,128)S(1)}, f32[768,128]{1,0:T(8,128)S(1)}, u32[]{:S(2)}, u32[]{:S(2)}) collective-permute-start(f32[768,128]{1,0:T(8,128)S(1)} %get-tuple-element.57.refs_2_), channel_id=1, source_target_pairs={{0,32},{16,48},{32,0},{48,16},{64,96},{80,112},{96,64},{112,80},{1... | collective-permute-start | bytes 1179656 | tf_op jit(solution)/shard_map/ppermute | solution.py:40
  51.4 3.4 %collective-permute-done.8 = f32[4,256,128]{2,1,0:T(8,128)S(1)} collective-permute-done((f32[4,256,128]{2,1,0:T(8,128)S(1)}, f32[4,256,128]{2,1,0:T(8,128)S(1)}, u32[]{:S(2)}, u32[]{:S(2)}) %collective-permute-start.8) | collective-permute-done | bytes 524320 | tf_op jit(solution)/shard_map/ppermute | solution.py:40
  54.8 0.3 shard_map.68
  55.0 0.7 collective-permute-start.13
  55.7 0.7 collective-permute-start.14
  56.4 0.0 collective-permute-done.6.refs_2_.refs_1_
  56.4 0.0 collective-permute-done.7.refs_3_.refs_2_
  56.5 1.3 %collective-permute-start.11 = (f32[256,128]{1,0:T(8,128)S(1)}, f32[256,128]{1,0:T(8,128)S(1)}, u32[]{:S(2)}, u32[]{:S(2)}) collective-permute-start(f32[256,128]{1,0:T(8,128)S(1)} %get-tuple-element.59.refs_4_), channel_id=1, source_target_pairs={{0,64},{16,80},{32,96},{48,112},{64,0},{80,16},{96,32},{112,48},{1... | collective-permute-start | bytes 393224 | tf_op jit(solution)/shard_map/ppermute | solution.py:40
  57.8 2.1 %collective-permute-start.12 = (f32[256,128]{1,0:T(8,128)S(1)}, f32[256,128]{1,0:T(8,128)S(1)}, u32[]{:S(2)}, u32[]{:S(2)}) collective-permute-start(f32[256,128]{1,0:T(8,128)S(1)} %get-tuple-element.60.refs_5_), channel_id=1, source_target_pairs={{0,192},{16,208},{32,224},{48,240},{64,128},{80,144},{96,160},{112... | collective-permute-start | bytes 393224 | tf_op jit(solution)/shard_map/ppermute | solution.py:40
  59.9 0.7 collective-permute-done.13.refs_2_.refs_6_
  60.6 1.6 %collective-permute-done.14.refs_3_.refs_7_ = f32[2,128,128]{2,1,0:T(8,128)S(1)} collective-permute-done((f32[2,128,128]{2,1,0:T(8,128)S(1)}, f32[2,128,128]{2,1,0:T(8,128)S(1)}, u32[]{:S(2)}, u32[]{:S(2)}) %collective-permute-start.14) | collective-permute-done | bytes 131104 | tf_op jit(solution)/shard_map/ppermute | solution.py:40
  62.2 0.1 collective-permute-start.15
  62.3 1.1 %collective-permute-start.16 = (f32[128,128]{1,0:T(8,128)S(1)}, f32[128,128]{1,0:T(8,128)S(1)}, u32[]{:S(2)}, u32[]{:S(2)}) collective-permute-start(f32[128,128]{1,0:T(8,128)S(1)} %get-tuple-element.66), channel_id=1, source_target_pairs={{0,192},{16,208},{32,224},{48,240},{64,128},{80,144},{96,160},{112... | collective-permute-start | bytes 196616 | tf_op jit(solution)/shard_map/ppermute | solution.py:40
  63.4 3.2 %collective-permute-done.15.refs_8_ = f32[128,128]{1,0:T(8,128)S(1)} collective-permute-done((f32[128,128]{1,0:T(8,128)S(1)}, f32[128,128]{1,0:T(8,128)S(1)}, u32[]{:S(2)}, u32[]{:S(2)}) %collective-permute-start.15) | collective-permute-done | bytes 65568 | tf_op jit(solution)/shard_map/ppermute | solution.py:40
  66.5 1.3 %collective-permute-done.16.refs_9_ = f32[128,128]{1,0:T(8,128)S(1)} collective-permute-done((f32[128,128]{1,0:T(8,128)S(1)}, f32[128,128]{1,0:T(8,128)S(1)}, u32[]{:S(2)}, u32[]{:S(2)}) %collective-permute-start.16) | collective-permute-done | bytes 65568 | tf_op jit(solution)/shard_map/ppermute | solution.py:40
  67.8 0.0 collective-permute-done.11.refs_3_
  67.8 0.0 collective-permute-done.12.refs_4_
  67.8 0.0 collective-permute-done.17.refs_11_
  67.9 0.5 shard_map.71
  68.3 22.5 %all_to_all.5.pieces_ref = bf16[16,96,128]{2,1,0:T(8,128)(2,1)} all-to-all(bf16[16,96,128]{2,1,0:T(8,128)(2,1)S(1)} %shard_map.71), channel_id=1, replica_groups=mesh['intra'=16,'inter'=16] {'inter'}, dimensions={0} | all-to-all | bytes 786432 | tf_op jit(solution)/shard_map/all_to_all | solution.py:273
  90.8 1.7 %shard_map.72 = (f32[8,768]{1,0:T(8,128)}, f32[8,768]{1,0:T(8,128)}) custom-call(bf16[16,96,128]{2,1,0:T(8,128)(2,1)} %all_to_all.5.pieces_ref), custom_call_target="tpu_custom_call" | custom-call | tf_op jit(solution)/shard_map/pallas_call | solution.py:275
  (9 shorter events, 0.1 us)
Async XLA Ops:
  0.6 0.8 copy-start.2
  1.4 6.0 %copy-start = (bf16[128,12288]{1,0:T(8,128)(2,1)S(1)}, bf16[128,12288]{1,0:T(8,128)(2,1)}, u32[]{:S(2)}) copy-start(bf16[128,12288]{1,0:T(8,128)(2,1)} %upstream_ref.5) | copy-start | bytes 9437188
  1.4 6.0 %copy-start.1 = (bf16[128,128]{1,0:T(8,128)(2,1)S(1)}, bf16[128,128]{1,0:T(8,128)(2,1)}, u32[]{:S(2)}) copy-start(bf16[128,128]{1,0:T(8,128)(2,1)} %hidden_ref.5) | copy-start | bytes 98308
  7.3 5.0 %collective-permute-start.1 = (bf16[8,768,128]{2,1,0:T(8,128)(2,1)S(1)}, bf16[8,768,128]{2,1,0:T(8,128)(2,1)S(1)}, u32[]{:S(2)}, u32[]{:S(2)}) collective-permute-start(bf16[8,768,128]{2,1,0:T(8,128)(2,1)S(1)} %get-tuple-element.38), channel_id=1, source_target_pairs={{0,16},{16,0},{32,48},{48,32},{64,80},{80,64},{96,112},{112,96},{1... | collective-permute-start | bytes 4718600 | tf_op jit(solution)/shard_map/ppermute | solution.py:40
  11.7 5.0 %collective-permute-start = (bf16[8,512,128]{2,1,0:T(8,128)(2,1)S(1)}, bf16[8,512,128]{2,1,0:T(8,128)(2,1)S(1)}, u32[]{:S(2)}, u32[]{:S(2)}) collective-permute-start(bf16[8,512,128]{2,1,0:T(8,128)(2,1)S(1)} %get-tuple-element.36), channel_id=1, source_target_pairs={{0,16},{16,0},{32,48},{48,32},{64,80},{80,64},{96,112},{112,96},{1... | collective-permute-start | bytes 3145736 | tf_op jit(solution)/shard_map/ppermute | solution.py:40
  13.1 19.6 %collective-permute-start.3 = (f32[2,768,128]{2,1,0:T(8,128)S(1)}, f32[2,768,128]{2,1,0:T(8,128)S(1)}, u32[]{:S(2)}, u32[]{:S(2)}) collective-permute-start(f32[2,768,128]{2,1,0:T(8,128)S(1)} %get-tuple-element.44), channel_id=1, source_target_pairs={{0,64},{16,80},{32,96},{48,112},{64,0},{80,16},{96,32},{112,48},{1... | collective-permute-start | bytes 2359304 | tf_op jit(solution)/shard_map/ppermute | solution.py:40
  14.7 20.4 %collective-permute-start.4 = (f32[2,768,128]{2,1,0:T(8,128)S(1)}, f32[2,768,128]{2,1,0:T(8,128)S(1)}, u32[]{:S(2)}, u32[]{:S(2)}) collective-permute-start(f32[2,768,128]{2,1,0:T(8,128)S(1)} %get-tuple-element.45), channel_id=1, source_target_pairs={{0,192},{16,208},{32,224},{48,240},{64,128},{80,144},{96,160},{112... | collective-permute-start | bytes 2359304 | tf_op jit(solution)/shard_map/ppermute | solution.py:40
  17.3 26.2 %collective-permute-start.2 = (f32[4,512,128]{2,1,0:T(8,128)S(1)}, f32[4,512,128]{2,1,0:T(8,128)S(1)}, u32[]{:S(2)}, u32[]{:S(2)}) collective-permute-start(f32[4,512,128]{2,1,0:T(8,128)S(1)} %get-tuple-element.41), channel_id=1, source_target_pairs={{0,32},{16,48},{32,0},{48,16},{64,96},{80,112},{96,64},{112,80},{1... | collective-permute-start | bytes 3145736 | tf_op jit(solution)/shard_map/ppermute | solution.py:40
  22.2 2.0 %collective-permute-start.5 = (bf16[8,256,128]{2,1,0:T(8,128)(2,1)S(1)}, bf16[8,256,128]{2,1,0:T(8,128)(2,1)S(1)}, u32[]{:S(2)}, u32[]{:S(2)}) collective-permute-start(bf16[8,256,128]{2,1,0:T(8,128)(2,1)S(1)} %get-tuple-element.47), channel_id=1, source_target_pairs={{0,16},{16,0},{32,48},{48,32},{64,80},{80,64},{96,112},{112,96},{1... | collective-permute-start | bytes 1572872 | tf_op jit(solution)/shard_map/ppermute | solution.py:40
  35.2 12.3 %collective-permute-start.10 = (f32[768,128]{1,0:T(8,128)S(1)}, f32[768,128]{1,0:T(8,128)S(1)}, u32[]{:S(2)}, u32[]{:S(2)}) collective-permute-start(f32[768,128]{1,0:T(8,128)S(1)} %get-tuple-element.50.refs_3_), channel_id=1, source_target_pairs={{0,192},{16,208},{32,224},{48,240},{64,128},{80,144},{96,160},{112... | collective-permute-start | bytes 1179656 | tf_op jit(solution)/shard_map/ppermute | solution.py:40
  37.3 12.1 %collective-permute-start.9 = (f32[768,128]{1,0:T(8,128)S(1)}, f32[768,128]{1,0:T(8,128)S(1)}, u32[]{:S(2)}, u32[]{:S(2)}) collective-permute-start(f32[768,128]{1,0:T(8,128)S(1)} %get-tuple-element.49.refs_2_), channel_id=1, source_target_pairs={{0,64},{16,80},{32,96},{48,112},{64,0},{80,16},{96,32},{112,48},{1... | collective-permute-start | bytes 1179656 | tf_op jit(solution)/shard_map/ppermute | solution.py:40
  37.3 17.4 %collective-permute-start.8 = (f32[4,256,128]{2,1,0:T(8,128)S(1)}, f32[4,256,128]{2,1,0:T(8,128)S(1)}, u32[]{:S(2)}, u32[]{:S(2)}) collective-permute-start(f32[4,256,128]{2,1,0:T(8,128)S(1)} %get-tuple-element.48.refs_4_), channel_id=1, source_target_pairs={{0,32},{16,48},{32,0},{48,16},{64,96},{80,112},{96,64},{112,80},{1... | collective-permute-start | bytes 1572872 | tf_op jit(solution)/shard_map/ppermute | solution.py:40
  43.9 12.5 %collective-permute-start.6 = (f32[2,256,128]{2,1,0:T(8,128)S(1)}, f32[2,256,128]{2,1,0:T(8,128)S(1)}, u32[]{:S(2)}, u32[]{:S(2)}) collective-permute-start(f32[2,256,128]{2,1,0:T(8,128)S(1)} %get-tuple-element.52), channel_id=1, source_target_pairs={{0,64},{16,80},{32,96},{48,112},{64,0},{80,16},{96,32},{112,48},{1... | collective-permute-start | bytes 786440 | tf_op jit(solution)/shard_map/ppermute | solution.py:40
  44.6 11.8 %collective-permute-start.7 = (f32[2,256,128]{2,1,0:T(8,128)S(1)}, f32[2,256,128]{2,1,0:T(8,128)S(1)}, u32[]{:S(2)}, u32[]{:S(2)}) collective-permute-start(f32[2,256,128]{2,1,0:T(8,128)S(1)} %get-tuple-element.53), channel_id=1, source_target_pairs={{0,192},{16,208},{32,224},{48,240},{64,128},{80,144},{96,160},{112... | collective-permute-start | bytes 786440 | tf_op jit(solution)/shard_map/ppermute | solution.py:40
  49.7 18.1 %collective-permute-start.17 = (f32[768,128]{1,0:T(8,128)S(1)}, f32[768,128]{1,0:T(8,128)S(1)}, u32[]{:S(2)}, u32[]{:S(2)}) collective-permute-start(f32[768,128]{1,0:T(8,128)S(1)} %get-tuple-element.57.refs_2_), channel_id=1, source_target_pairs={{0,32},{16,48},{32,0},{48,16},{64,96},{80,112},{96,64},{112,80},{1... | collective-permute-start | bytes 1179656 | tf_op jit(solution)/shard_map/ppermute | solution.py:40
  55.0 5.5 %collective-permute-start.13 = (f32[2,128,128]{2,1,0:T(8,128)S(1)}, f32[2,128,128]{2,1,0:T(8,128)S(1)}, u32[]{:S(2)}, u32[]{:S(2)}) collective-permute-start(f32[2,128,128]{2,1,0:T(8,128)S(1)} %get-tuple-element.61), channel_id=1, source_target_pairs={{0,64},{16,80},{32,96},{48,112},{64,0},{80,16},{96,32},{112,48},{1... | collective-permute-start | bytes 393224 | tf_op jit(solution)/shard_map/ppermute | solution.py:40
  55.7 6.4 %collective-permute-start.14 = (f32[2,128,128]{2,1,0:T(8,128)S(1)}, f32[2,128,128]{2,1,0:T(8,128)S(1)}, u32[]{:S(2)}, u32[]{:S(2)}) collective-permute-start(f32[2,128,128]{2,1,0:T(8,128)S(1)} %get-tuple-element.62), channel_id=1, source_target_pairs={{0,192},{16,208},{32,224},{48,240},{64,128},{80,144},{96,160},{112... | collective-permute-start | bytes 393224 | tf_op jit(solution)/shard_map/ppermute | solution.py:40
  56.5 11.4 %collective-permute-start.11 = (f32[256,128]{1,0:T(8,128)S(1)}, f32[256,128]{1,0:T(8,128)S(1)}, u32[]{:S(2)}, u32[]{:S(2)}) collective-permute-start(f32[256,128]{1,0:T(8,128)S(1)} %get-tuple-element.59.refs_4_), channel_id=1, source_target_pairs={{0,64},{16,80},{32,96},{48,112},{64,0},{80,16},{96,32},{112,48},{1... | collective-permute-start | bytes 393224 | tf_op jit(solution)/shard_map/ppermute | solution.py:40
  57.8 10.1 %collective-permute-start.12 = (f32[256,128]{1,0:T(8,128)S(1)}, f32[256,128]{1,0:T(8,128)S(1)}, u32[]{:S(2)}, u32[]{:S(2)}) collective-permute-start(f32[256,128]{1,0:T(8,128)S(1)} %get-tuple-element.60.refs_5_), channel_id=1, source_target_pairs={{0,192},{16,208},{32,224},{48,240},{64,128},{80,144},{96,160},{112... | collective-permute-start | bytes 393224 | tf_op jit(solution)/shard_map/ppermute | solution.py:40
  62.2 4.4 %collective-permute-start.15 = (f32[128,128]{1,0:T(8,128)S(1)}, f32[128,128]{1,0:T(8,128)S(1)}, u32[]{:S(2)}, u32[]{:S(2)}) collective-permute-start(f32[128,128]{1,0:T(8,128)S(1)} %get-tuple-element.65), channel_id=1, source_target_pairs={{0,64},{16,80},{32,96},{48,112},{64,0},{80,16},{96,32},{112,48},{1... | collective-permute-start | bytes 196616 | tf_op jit(solution)/shard_map/ppermute | solution.py:40
  62.3 5.6 %collective-permute-start.16 = (f32[128,128]{1,0:T(8,128)S(1)}, f32[128,128]{1,0:T(8,128)S(1)}, u32[]{:S(2)}, u32[]{:S(2)}) collective-permute-start(f32[128,128]{1,0:T(8,128)S(1)} %get-tuple-element.66), channel_id=1, source_target_pairs={{0,192},{16,208},{32,224},{48,240},{64,128},{80,144},{96,160},{112... | collective-permute-start | bytes 196616 | tf_op jit(solution)/shard_map/ppermute | solution.py:40
where the time goes:
time: 92.7 us; the launch traced here: 92.5 us
  waiting for transfers between devices  31.2 us (34%)
  blocking collectives  22.5 us (24%)
  starting transfers between devices  18.9 us (20%)
  Pallas kernels  18.3 us (20%)
    ppermute x18, waiting for transfers between devices, send(): return lax.ppermute(array, 'intra', pairs)  31.2 us
    all_to_all x1, blocking collectives, body(): lax.all_to_all(node, 'inter', split_axis=0, concat_axis=0, tiled=True)  22.5 us
    ppermute x18, starting transfers between devices, send(): return lax.ppermute(array, 'intra', pairs)  18.9 us
    pallas_call x3, Pallas kernels, gradients(): pl.pallas_call(functools.partial(gradient_kernel, share, along_y_first, l...  13.4 us
    pallas_call x9, Pallas kernels, tiled_call(): pl.pallas_call(kernel, grid=(steps,), in_specs=[spec(a.shape) for a in in...  2.82 us
  transfers between devices with their start and end apart: 18, of which 11 were waited for; matrix products, arithmetic and copies ran while one was open for 0% of the time, Pallas kernels for 11%

commit v1 on v0

--- a/solution.py
+++ b/solution.py
@@ -33,6 +33,7 @@
 TO_CORE = node_pairs(lambda x, y, core: (x, y, 1 - core))
 TO_Y = node_pairs(lambda x, y, core: (x, 1 - y, core))
 TO_FIRST = node_pairs(lambda x, y, core: (x + 1 - 2 * (x % 2), y, core))
+TO_FAR = node_pairs(lambda x, y, core: (x + 2, y, core))
 TO_SECOND = node_pairs(lambda x, y, core: (x - 1 + 2 * (x % 2), y, core))
 
 
@@ -132,23 +133,27 @@
 
 
 def tiled_call(kernel, steps, ins, outs, after=()):
-    if after:
-        inner = kernel
-
-        def kernel(*refs):
-            inner(*refs[: len(ins)], *refs[len(ins) + len(after) :])
-
-    def spec(shape):
-        tile = shape[-2] // steps
-        lead = len(shape) - 2
-        return pl.BlockSpec(shape[:-2] + (tile, BLOCK), lambda c: (0,) * lead + (c, 0))
-
     shapes = [jax.ShapeDtypeStruct(tuple(lead) + (rows, BLOCK), dtype) for lead, rows, dtype in outs]
+
+    def view(ref, step):
+        tile = ref.shape[-2] // steps
+        rows = pl.ds(pl.multiple_of(step * tile, tile), tile)
+        return ref.at[(slice(None),) * (len(ref.shape) - 2) + (rows, slice(None))]
+
+    def whole(*refs):
+        used = refs[: len(ins)] + refs[len(ins) + len(after) :]
+
+        def one_step(step, carry):
+            kernel(*[view(ref, step) for ref in used])
+            return carry
+
+        lax.fori_loop(0, steps, one_step, 0)
+
     return pl.pallas_call(
-        kernel,
-        grid=(steps,),
-        in_specs=[spec(a.shape) for a in ins] + [pl.BlockSpec(memory_space=pl.ANY)] * len(after),
-        out_specs=[spec(s.shape) for s in shapes],
+        whole if steps > 1 else lambda *refs: kernel(*refs[: len(ins)], *refs[len(ins) + len(after) :]),
+        in_specs=[pl.BlockSpec(memory_space=pltpu.VMEM)] * len(ins)
+        + [pl.BlockSpec(memory_space=pl.ANY)] * len(after),
+        out_specs=[pl.BlockSpec(memory_space=pltpu.VMEM)] * len(shapes),
         out_shape=shapes,
         compiler_params=PARAMS,
         cost_estimate=SMALL,
@@ -176,6 +181,18 @@
     second_later_ref[...] = total(3, 0)
 
 
+def add_once_kernel(
+    keep_ref, got_ref, first_ref, second_ref, from_first_ref, from_second_ref, own_ref, to_first_ref, far_ref, to_second_ref
+):
+    ahead = first_ref.shape[0]
+    to_first_ref[:ahead] = first_ref[...] + from_second_ref[0]
+    to_second_ref[:ahead] = second_ref[...] + from_first_ref[0]
+    own_ref[...] = up(keep_ref, 0) + up(got_ref, 0)
+    to_first_ref[ahead:] = up(keep_ref, 1) + up(got_ref, 1)
+    far_ref[...] = up(keep_ref, 2) + up(got_ref, 2)
+    to_second_ref[ahead:] = up(keep_ref, 3) + up(got_ref, 3)
+
+
 def fold_kernel(first_ref, second_ref, from_first_ref, from_second_ref, to_first_ref, to_second_ref):
     to_first_ref[...] = first_ref[...] + from_second_ref[0]
     to_second_ref[...] = second_ref[...] + from_first_ref[0]
@@ -193,11 +210,16 @@
 
 def nodes_kernel(*refs):
     out_ref = refs[-1]
-    parts = []
-    for share in (refs[:5], refs[5:10]):
-        parts.append(jnp.concatenate([round_to_step(half).astype(jnp.bfloat16) for half in halves(*share)], axis=0))
-    stay_ref, got_ref = refs[10:12]
-    parts.append(round_to_step(stay_ref[...] + got_ref[...]).astype(jnp.bfloat16))
+    own_a_ref, from_first_ref, from_second_ref, own_c_ref, first_ref, second_ref, far_ref, stay_ref, got_ref = refs[:-1]
+    ahead = own_a_ref.shape[1]
+    a = (
+        own_a_ref[0] + from_first_ref[1] + second_ref[:ahead],
+        own_a_ref[1] + from_second_ref[1] + first_ref[:ahead],
+    )
+    a = jnp.concatenate([round_to_step(half).astype(jnp.bfloat16) for half in a], axis=0)
+    c = own_c_ref[...] + first_ref[ahead:] + far_ref[...] + second_ref[ahead:]
+    b = stay_ref[...] + got_ref[...]
+    parts = [a, round_to_step(c).astype(jnp.bfloat16), round_to_step(b).astype(jnp.bfloat16)]
     at = 0
     for part in parts:
         rows = part.shape[0] // OWNERS
@@ -260,19 +282,28 @@
     a = start_x(halved(stay_a, 4), halved(y_a, 4), sent_b)
     stay_b, go_b = tiled_call(node_pairs_kernel, 2, b, [((), b[0].shape[1], f32)] * 2, (a[0],))
     y_b = send(go_b, TO_Y)
-    c = start_x(halved(stay_c, 4), halved(y_c, 4), (go_b,))
-    a, sent_a = end_x(*a, (c[0],))
-    c, _ = end_x(*c, sent_a)
+    rows, ahead = stay_c.shape[1], a[1].shape[0]
+    own_c, first, far, second = tiled_call(
+        add_once_kernel,
+        1,
+        (stay_c, y_c, *a[1:]),
+        [((), rows, f32), ((), ahead + rows, f32), ((), rows, f32), ((), ahead + rows, f32)],
+        (go_b,),
+    )
+    first, second, far = send(first, TO_FIRST), send(second, TO_SECOND), send(far, TO_FAR)
 
     node = pl.pallas_call(
         nodes_kernel,
+        in_specs=[pl.BlockSpec(memory_space=pltpu.VMEM)] * 9,
+        out_specs=pl.BlockSpec(memory_space=pltpu.VMEM),
         out_shape=jax.ShapeDtypeStruct((OWNERS, 2 * LAYER * SHARE, BLOCK), bf16),
         compiler_params=PARAMS,
         cost_estimate=SMALL,
-    )(*a, *c, stay_b, y_b)
+    )(a[0], a[3], a[4], own_c, first, second, far, stay_b, y_b)
     pieces = lax.all_to_all(node, "inter", split_axis=0, concat_axis=0, tiled=True)
     out = jax.ShapeDtypeStruct((SHARE, LAYER * BLOCK), f32)
-    return pl.pallas_call(final_kernel, out_shape=(out, out))(pieces)
+    vmem = pl.BlockSpec(memory_space=pltpu.VMEM)
+    return pl.pallas_call(final_kernel, in_specs=[vmem], out_shape=(out, out))(pieces)
 
 
 def solution(mesh):

time: 92.7 us -> 91.1 us (0.983)
  waiting for transfers between devices: 31.2 us -> 33.3 us
  starting transfers between devices: 18.9 us -> 17.1 us
  Pallas kernels: 18.3 us -> 16.6 us
    ppermute x18 -> x15, waiting for transfers between devices: 31.2 us -> 33.3 us  [send(): return lax.ppermute(array, 'intra', pairs)]
    pallas_call x11 -> x9, Pallas kernels: 4.94 us -> 3.15 us  [the longest x1 1.67 us: body(): pl.pallas_call(final_kernel, in_specs=[vmem], out_shape=(out, out))(pieces)]
    ppermute x18 -> x15, starting transfers between devices: 18.9 us -> 17.1 us  [send(): return lax.ppermute(array, 'intra', pairs)]
  transfers between devices with their start and end apart: 18 -> 15, of which waited for: 11 -> 10; matrix products, arithmetic and copies ran while one was open for 0% -> 0% of each run, Pallas kernels for 11% -> 9%
where the time goes in v1:
time: 91.1 us; the launch traced here: 90.8 us
  waiting for transfers between devices  33.3 us (37%)
  blocking collectives  22.3 us (24%)
  starting transfers between devices  17.1 us (19%)
  Pallas kernels  16.6 us (18%)
    ppermute x15, waiting for transfers between devices, send(): return lax.ppermute(array, 'intra', pairs)  33.3 us
    all_to_all x1, blocking collectives, body(): lax.all_to_all(node, 'inter', split_axis=0, concat_axis=0, tiled=True)  22.3 us
    ppermute x15, starting transfers between devices, send(): return lax.ppermute(array, 'intra', pairs)  17.1 us
    pallas_call x3, Pallas kernels, gradients(): pl.pallas_call(functools.partial(gradient_kernel, share, along_y_first, l...  13.4 us
  transfers between devices with their start and end apart: 15, of which 10 were waited for; matrix products, arithmetic and copies ran while one was open for 0% of the time, Pallas kernels for 9%

profile of v1, /device:TPU:32, one launch (start us, length us, event | category | flops | bytes accessed | tf_op | source)
XLA Modules:
  0.0 90.8 jit_solution(18128837353390866570)
XLA Ops:
  0.6 0.0 copy-start.2
  0.6 0.7 copy-done.2
  1.4 0.0 copy-start.1
  1.4 5.9 %shard_map.60 = (bf16[8,768,128]{2,1,0:T(8,128)(2,1)S(1)}, bf16[8,768,128]{2,1,0:T(8,128)(2,1)S(1)}) custom-call(s32[1]{0:T(128)} %bitcast.me_ref, bf16[128,128]{1,0:T(8,128)(2,1)S(1)} %copy-done.2, bf16[128,12288]{1,0:T(8,128)(2,1)} %upstream_ref.4), custom_call_target="tpu_custom_call" | custom-call | flops 1 | bytes 1 | tf_op jit(solution)/shard_map/pallas_call | solution.py:116
  7.3 0.1 collective-permute-start.1
  7.4 0.0 copy-done
  7.4 0.0 copy-done.1
  7.4 4.3 %shard_map.59 = (bf16[8,512,128]{2,1,0:T(8,128)(2,1)S(1)}, bf16[8,512,128]{2,1,0:T(8,128)(2,1)S(1)}) custom-call(s32[1]{0:T(128)} %bitcast.me_ref, bf16[128,128]{1,0:T(8,128)(2,1)S(1)} %copy-done.1, bf16[128,12288]{1,0:T(8,128)(2,1)S(1)} %copy-done), custom_call_target="tpu_custom_call" | custom-call | flops 1 | bytes 1 | tf_op jit(solution)/shard_map/pallas_call | solution.py:116
  11.7 0.6 collective-permute-start
  12.3 0.0 collective-permute-done.1
  12.3 0.3 shard_map.61
  12.6 2.0 %collective-permute-done.refs_1_ = bf16[8,512,128]{2,1,0:T(8,128)(2,1)S(1)} collective-permute-done((bf16[8,512,128]{2,1,0:T(8,128)(2,1)S(1)}, bf16[8,512,128]{2,1,0:T(8,128)(2,1)S(1)}, u32[]{:S(2)}, u32[]{:S(2)}) %collective-permute-start) | collective-permute-done | bytes 1048608 | tf_op jit(solution)/shard_map/ppermute | solution.py:41
  14.6 0.2 shard_map.62
  14.8 1.7 %collective-permute-start.2 = (f32[4,512,128]{2,1,0:T(8,128)S(1)}, f32[4,512,128]{2,1,0:T(8,128)S(1)}, u32[]{:S(2)}, u32[]{:S(2)}) collective-permute-start(f32[4,512,128]{2,1,0:T(8,128)S(1)} %get-tuple-element.36), channel_id=1, source_target_pairs={{0,32},{16,48},{32,0},{48,16},{64,96},{80,112},{96,64},{112,80},{1... | collective-permute-start | bytes 3145736 | tf_op jit(solution)/shard_map/ppermute | solution.py:41
  16.5 1.5 %collective-permute-start.3 = (f32[2,768,128]{2,1,0:T(8,128)S(1)}, f32[2,768,128]{2,1,0:T(8,128)S(1)}, u32[]{:S(2)}, u32[]{:S(2)}) collective-permute-start(f32[2,768,128]{2,1,0:T(8,128)S(1)} %get-tuple-element.39), channel_id=1, source_target_pairs={{0,64},{16,80},{32,96},{48,112},{64,0},{80,16},{96,32},{112,48},{1... | collective-permute-start | bytes 2359304 | tf_op jit(solution)/shard_map/ppermute | solution.py:41
  18.0 2.1 %collective-permute-start.4 = (f32[2,768,128]{2,1,0:T(8,128)S(1)}, f32[2,768,128]{2,1,0:T(8,128)S(1)}, u32[]{:S(2)}, u32[]{:S(2)}) collective-permute-start(f32[2,768,128]{2,1,0:T(8,128)S(1)} %get-tuple-element.40), channel_id=1, source_target_pairs={{0,192},{16,208},{32,224},{48,240},{64,128},{80,144},{96,160},{112... | collective-permute-start | bytes 2359304 | tf_op jit(solution)/shard_map/ppermute | solution.py:41
  20.1 3.2 %shard_map.63 = (bf16[8,256,128]{2,1,0:T(8,128)(2,1)S(1)}, bf16[8,256,128]{2,1,0:T(8,128)(2,1)S(1)}) custom-call(s32[1]{0:T(128)} %bitcast.me_ref, bf16[128,128]{1,0:T(8,128)(2,1)S(1)} %copy-done.1, bf16[128,12288]{1,0:T(8,128)(2,1)S(1)} %copy-done, f32[4,512,128]{2,1,0:T(8,128)S(1)} %get-tuple-element.35.refs_0_), custom_call_target="tpu_custom_call" | custom-call | flops 1 | bytes 1 | tf_op jit(solution)/shard_map/pallas_call | solution.py:116
  23.3 0.1 collective-permute-start.5
  23.4 1.9 %collective-permute-done.5.refs_1_ = bf16[8,256,128]{2,1,0:T(8,128)(2,1)S(1)} collective-permute-done((bf16[8,256,128]{2,1,0:T(8,128)(2,1)S(1)}, bf16[8,256,128]{2,1,0:T(8,128)(2,1)S(1)}, u32[]{:S(2)}, u32[]{:S(2)}) %collective-permute-start.5) | collective-permute-done | bytes 524320 | tf_op jit(solution)/shard_map/ppermute | solution.py:41
  25.3 0.1 shard_map.64
  25.4 0.5 collective-permute-start.8
  25.9 10.1 %collective-permute-done.3.refs_2_.refs_1_ = f32[2,768,128]{2,1,0:T(8,128)S(1)} collective-permute-done((f32[2,768,128]{2,1,0:T(8,128)S(1)}, f32[2,768,128]{2,1,0:T(8,128)S(1)}, u32[]{:S(2)}, u32[]{:S(2)}) %collective-permute-start.3) | collective-permute-done | bytes 786464 | tf_op jit(solution)/shard_map/ppermute | solution.py:41
  36.0 2.4 %collective-permute-done.4.refs_3_.refs_2_ = f32[2,768,128]{2,1,0:T(8,128)S(1)} collective-permute-done((f32[2,768,128]{2,1,0:T(8,128)S(1)}, f32[2,768,128]{2,1,0:T(8,128)S(1)}, u32[]{:S(2)}, u32[]{:S(2)}) %collective-permute-start.4) | collective-permute-done | bytes 786464 | tf_op jit(solution)/shard_map/ppermute | solution.py:41
  38.4 0.1 shard_map.65
  38.5 2.2 %collective-permute-start.10 = (f32[768,128]{1,0:T(8,128)S(1)}, f32[768,128]{1,0:T(8,128)S(1)}, u32[]{:S(2)}, u32[]{:S(2)}) collective-permute-start(f32[768,128]{1,0:T(8,128)S(1)} %get-tuple-element.45.refs_3_), channel_id=1, source_target_pairs={{0,192},{16,208},{32,224},{48,240},{64,128},{80,144},{96,160},{112... | collective-permute-start | bytes 1179656 | tf_op jit(solution)/shard_map/ppermute | solution.py:41
  40.7 0.0 collective-permute-start.9
  40.7 0.2 collective-permute-done.2
  40.9 0.1 shard_map.66
  41.0 1.9 %collective-permute-start.6 = (f32[2,256,128]{2,1,0:T(8,128)S(1)}, f32[2,256,128]{2,1,0:T(8,128)S(1)}, u32[]{:S(2)}, u32[]{:S(2)}) collective-permute-start(f32[2,256,128]{2,1,0:T(8,128)S(1)} %get-tuple-element.47), channel_id=1, source_target_pairs={{0,64},{16,80},{32,96},{48,112},{64,0},{80,16},{96,32},{112,48},{1... | collective-permute-start | bytes 786440 | tf_op jit(solution)/shard_map/ppermute | solution.py:41
  42.9 1.7 %collective-permute-start.7 = (f32[2,256,128]{2,1,0:T(8,128)S(1)}, f32[2,256,128]{2,1,0:T(8,128)S(1)}, u32[]{:S(2)}, u32[]{:S(2)}) collective-permute-start(f32[2,256,128]{2,1,0:T(8,128)S(1)} %get-tuple-element.48), channel_id=1, source_target_pairs={{0,192},{16,208},{32,224},{48,240},{64,128},{80,144},{96,160},{112... | collective-permute-start | bytes 786440 | tf_op jit(solution)/shard_map/ppermute | solution.py:41
  44.7 7.2 %collective-permute-done.10.refs_4_ = f32[768,128]{1,0:T(8,128)S(1)} collective-permute-done((f32[768,128]{1,0:T(8,128)S(1)}, f32[768,128]{1,0:T(8,128)S(1)}, u32[]{:S(2)}, u32[]{:S(2)}) %collective-permute-start.10) | collective-permute-done | bytes 393248 | tf_op jit(solution)/shard_map/ppermute | solution.py:41
  51.9 0.9 collective-permute-done.9.refs_3_
  52.7 0.1 shard_map.67
  52.9 0.5 collective-permute-start.14
  53.4 0.0 collective-permute-done.8.refs_1_
  53.4 2.6 %collective-permute-done.6.refs_4_.refs_1_ = f32[2,256,128]{2,1,0:T(8,128)S(1)} collective-permute-done((f32[2,256,128]{2,1,0:T(8,128)S(1)}, f32[2,256,128]{2,1,0:T(8,128)S(1)}, u32[]{:S(2)}, u32[]{:S(2)}) %collective-permute-start.6) | collective-permute-done | bytes 262176 | tf_op jit(solution)/shard_map/ppermute | solution.py:41
  56.0 0.0 collective-permute-done.7.refs_5_.refs_2_
  56.0 0.1 shard_map.68
  56.1 0.4 collective-permute-start.11
  56.4 1.3 %collective-permute-start.12 = (f32[512,128]{1,0:T(8,128)S(1)}, f32[512,128]{1,0:T(8,128)S(1)}, u32[]{:S(2)}, u32[]{:S(2)}) collective-permute-start(f32[512,128]{1,0:T(8,128)S(1)} %get-tuple-element.55), channel_id=1, source_target_pairs={{0,192},{16,208},{32,224},{48,240},{64,128},{80,144},{96,160},{112... | collective-permute-start | bytes 786440 | tf_op jit(solution)/shard_map/ppermute | solution.py:41
  57.7 2.5 %collective-permute-start.13 = (f32[256,128]{1,0:T(8,128)S(1)}, f32[256,128]{1,0:T(8,128)S(1)}, u32[]{:S(2)}, u32[]{:S(2)}) collective-permute-start(f32[256,128]{1,0:T(8,128)S(1)} %get-tuple-element.56), channel_id=1, source_target_pairs={{0,128},{16,144},{32,160},{48,176},{64,192},{80,208},{96,224},{112... | collective-permute-start | bytes 393224 | tf_op jit(solution)/shard_map/ppermute | solution.py:41
  60.2 6.0 %collective-permute-done.13.refs_6_ = f32[256,128]{1,0:T(8,128)S(1)} collective-permute-done((f32[256,128]{1,0:T(8,128)S(1)}, f32[256,128]{1,0:T(8,128)S(1)}, u32[]{:S(2)}, u32[]{:S(2)}) %collective-permute-start.13) | collective-permute-done | bytes 131104 | tf_op jit(solution)/shard_map/ppermute | solution.py:41
  66.2 0.0 collective-permute-done.11.refs_4_
  66.2 0.2 collective-permute-done.12.refs_5_
  66.4 0.0 collective-permute-done.14.refs_8_
  66.4 0.4 shard_map.69
  66.8 22.3 %all_to_all.5.pieces_ref = bf16[16,96,128]{2,1,0:T(8,128)(2,1)} all-to-all(bf16[16,96,128]{2,1,0:T(8,128)(2,1)S(1)} %shard_map.69), channel_id=1, replica_groups=mesh['intra'=16,'inter'=16] {'inter'}, dimensions={0} | all-to-all | bytes 786432 | tf_op jit(solution)/shard_map/all_to_all | solution.py:303
  89.2 1.7 %shard_map.70 = (f32[8,768]{1,0:T(8,128)}, f32[8,768]{1,0:T(8,128)}) custom-call(bf16[16,96,128]{2,1,0:T(8,128)(2,1)} %all_to_all.5.pieces_ref), custom_call_target="tpu_custom_call" | custom-call | tf_op jit(solution)/shard_map/pallas_call | solution.py:306
  (1 shorter events, 0.0 us)
Async XLA Ops:
  0.6 0.8 copy-start.2
  1.4 6.0 %copy-start = (bf16[128,12288]{1,0:T(8,128)(2,1)S(1)}, bf16[128,12288]{1,0:T(8,128)(2,1)}, u32[]{:S(2)}) copy-start(bf16[128,12288]{1,0:T(8,128)(2,1)} %upstream_ref.5) | copy-start | bytes 9437188
  1.4 6.0 %copy-start.1 = (bf16[128,128]{1,0:T(8,128)(2,1)S(1)}, bf16[128,128]{1,0:T(8,128)(2,1)}, u32[]{:S(2)}) copy-start(bf16[128,128]{1,0:T(8,128)(2,1)} %hidden_ref.5) | copy-start | bytes 98308
  7.3 5.0 %collective-permute-start.1 = (bf16[8,768,128]{2,1,0:T(8,128)(2,1)S(1)}, bf16[8,768,128]{2,1,0:T(8,128)(2,1)S(1)}, u32[]{:S(2)}, u32[]{:S(2)}) collective-permute-start(bf16[8,768,128]{2,1,0:T(8,128)(2,1)S(1)} %get-tuple-element.33), channel_id=1, source_target_pairs={{0,16},{16,0},{32,48},{48,32},{64,80},{80,64},{96,112},{112,96},{1... | collective-permute-start | bytes 4718600 | tf_op jit(solution)/shard_map/ppermute | solution.py:41
  11.7 2.8 %collective-permute-start = (bf16[8,512,128]{2,1,0:T(8,128)(2,1)S(1)}, bf16[8,512,128]{2,1,0:T(8,128)(2,1)S(1)}, u32[]{:S(2)}, u32[]{:S(2)}) collective-permute-start(bf16[8,512,128]{2,1,0:T(8,128)(2,1)S(1)} %get-tuple-element.31), channel_id=1, source_target_pairs={{0,16},{16,0},{32,48},{48,32},{64,80},{80,64},{96,112},{112,96},{1... | collective-permute-start | bytes 3145736 | tf_op jit(solution)/shard_map/ppermute | solution.py:41
  14.8 26.1 %collective-permute-start.2 = (f32[4,512,128]{2,1,0:T(8,128)S(1)}, f32[4,512,128]{2,1,0:T(8,128)S(1)}, u32[]{:S(2)}, u32[]{:S(2)}) collective-permute-start(f32[4,512,128]{2,1,0:T(8,128)S(1)} %get-tuple-element.36), channel_id=1, source_target_pairs={{0,32},{16,48},{32,0},{48,16},{64,96},{80,112},{96,64},{112,80},{1... | collective-permute-start | bytes 3145736 | tf_op jit(solution)/shard_map/ppermute | solution.py:41
  16.5 19.5 %collective-permute-start.3 = (f32[2,768,128]{2,1,0:T(8,128)S(1)}, f32[2,768,128]{2,1,0:T(8,128)S(1)}, u32[]{:S(2)}, u32[]{:S(2)}) collective-permute-start(f32[2,768,128]{2,1,0:T(8,128)S(1)} %get-tuple-element.39), channel_id=1, source_target_pairs={{0,64},{16,80},{32,96},{48,112},{64,0},{80,16},{96,32},{112,48},{1... | collective-permute-start | bytes 2359304 | tf_op jit(solution)/shard_map/ppermute | solution.py:41
  18.0 20.5 %collective-permute-start.4 = (f32[2,768,128]{2,1,0:T(8,128)S(1)}, f32[2,768,128]{2,1,0:T(8,128)S(1)}, u32[]{:S(2)}, u32[]{:S(2)}) collective-permute-start(f32[2,768,128]{2,1,0:T(8,128)S(1)} %get-tuple-element.40), channel_id=1, source_target_pairs={{0,192},{16,208},{32,224},{48,240},{64,128},{80,144},{96,160},{112... | collective-permute-start | bytes 2359304 | tf_op jit(solution)/shard_map/ppermute | solution.py:41
  23.3 2.0 %collective-permute-start.5 = (bf16[8,256,128]{2,1,0:T(8,128)(2,1)S(1)}, bf16[8,256,128]{2,1,0:T(8,128)(2,1)S(1)}, u32[]{:S(2)}, u32[]{:S(2)}) collective-permute-start(bf16[8,256,128]{2,1,0:T(8,128)(2,1)S(1)} %get-tuple-element.42), channel_id=1, source_target_pairs={{0,16},{16,0},{32,48},{48,32},{64,80},{80,64},{96,112},{112,96},{1... | collective-permute-start | bytes 1572872 | tf_op jit(solution)/shard_map/ppermute | solution.py:41
  25.4 28.0 %collective-permute-start.8 = (f32[4,256,128]{2,1,0:T(8,128)S(1)}, f32[4,256,128]{2,1,0:T(8,128)S(1)}, u32[]{:S(2)}, u32[]{:S(2)}) collective-permute-start(f32[4,256,128]{2,1,0:T(8,128)S(1)} %get-tuple-element.43.refs_4_), channel_id=1, source_target_pairs={{0,32},{16,48},{32,0},{48,16},{64,96},{80,112},{96,64},{112,80},{1... | collective-permute-start | bytes 1572872 | tf_op jit(solution)/shard_map/ppermute | solution.py:41
  38.5 13.3 %collective-permute-start.10 = (f32[768,128]{1,0:T(8,128)S(1)}, f32[768,128]{1,0:T(8,128)S(1)}, u32[]{:S(2)}, u32[]{:S(2)}) collective-permute-start(f32[768,128]{1,0:T(8,128)S(1)} %get-tuple-element.45.refs_3_), channel_id=1, source_target_pairs={{0,192},{16,208},{32,224},{48,240},{64,128},{80,144},{96,160},{112... | collective-permute-start | bytes 1179656 | tf_op jit(solution)/shard_map/ppermute | solution.py:41
  40.7 12.1 %collective-permute-start.9 = (f32[768,128]{1,0:T(8,128)S(1)}, f32[768,128]{1,0:T(8,128)S(1)}, u32[]{:S(2)}, u32[]{:S(2)}) collective-permute-start(f32[768,128]{1,0:T(8,128)S(1)} %get-tuple-element.44.refs_2_), channel_id=1, source_target_pairs={{0,64},{16,80},{32,96},{48,112},{64,0},{80,16},{96,32},{112,48},{1... | collective-permute-start | bytes 1179656 | tf_op jit(solution)/shard_map/ppermute | solution.py:41
  41.0 15.0 %collective-permute-start.6 = (f32[2,256,128]{2,1,0:T(8,128)S(1)}, f32[2,256,128]{2,1,0:T(8,128)S(1)}, u32[]{:S(2)}, u32[]{:S(2)}) collective-permute-start(f32[2,256,128]{2,1,0:T(8,128)S(1)} %get-tuple-element.47), channel_id=1, source_target_pairs={{0,64},{16,80},{32,96},{48,112},{64,0},{80,16},{96,32},{112,48},{1... | collective-permute-start | bytes 786440 | tf_op jit(solution)/shard_map/ppermute | solution.py:41
  42.9 13.0 %collective-permute-start.7 = (f32[2,256,128]{2,1,0:T(8,128)S(1)}, f32[2,256,128]{2,1,0:T(8,128)S(1)}, u32[]{:S(2)}, u32[]{:S(2)}) collective-permute-start(f32[2,256,128]{2,1,0:T(8,128)S(1)} %get-tuple-element.48), channel_id=1, source_target_pairs={{0,192},{16,208},{32,224},{48,240},{64,128},{80,144},{96,160},{112... | collective-permute-start | bytes 786440 | tf_op jit(solution)/shard_map/ppermute | solution.py:41
  52.9 13.5 %collective-permute-start.14 = (f32[768,128]{1,0:T(8,128)S(1)}, f32[768,128]{1,0:T(8,128)S(1)}, u32[]{:S(2)}, u32[]{:S(2)}) collective-permute-start(f32[768,128]{1,0:T(8,128)S(1)} %get-tuple-element.52.refs_6_), channel_id=1, source_target_pairs={{0,32},{16,48},{32,0},{48,16},{64,96},{80,112},{96,64},{112,80},{1... | collective-permute-start | bytes 1179656 | tf_op jit(solution)/shard_map/ppermute | solution.py:41
  56.1 10.1 %collective-permute-start.11 = (f32[512,128]{1,0:T(8,128)S(1)}, f32[512,128]{1,0:T(8,128)S(1)}, u32[]{:S(2)}, u32[]{:S(2)}) collective-permute-start(f32[512,128]{1,0:T(8,128)S(1)} %get-tuple-element.54), channel_id=1, source_target_pairs={{0,64},{16,80},{32,96},{48,112},{64,0},{80,16},{96,32},{112,48},{1... | collective-permute-start | bytes 786440 | tf_op jit(solution)/shard_map/ppermute | solution.py:41
  56.4 9.9 %collective-permute-start.12 = (f32[512,128]{1,0:T(8,128)S(1)}, f32[512,128]{1,0:T(8,128)S(1)}, u32[]{:S(2)}, u32[]{:S(2)}) collective-permute-start(f32[512,128]{1,0:T(8,128)S(1)} %get-tuple-element.55), channel_id=1, source_target_pairs={{0,192},{16,208},{32,224},{48,240},{64,128},{80,144},{96,160},{112... | collective-permute-start | bytes 786440 | tf_op jit(solution)/shard_map/ppermute | solution.py:41
  57.7 8.5 %collective-permute-start.13 = (f32[256,128]{1,0:T(8,128)S(1)}, f32[256,128]{1,0:T(8,128)S(1)}, u32[]{:S(2)}, u32[]{:S(2)}) collective-permute-start(f32[256,128]{1,0:T(8,128)S(1)} %get-tuple-element.56), channel_id=1, source_target_pairs={{0,128},{16,144},{32,160},{48,176},{64,192},{80,208},{96,224},{112... | collective-permute-start | bytes 393224 | tf_op jit(solution)/shard_map/ppermute | solution.py:41

commit v2 on v1

--- a/solution.py
+++ b/solution.py
@@ -15,7 +15,7 @@
 STEPS = OWNERS // 2
 LAYER = 6
 FIRST = 4
-ROOM = (50, 46, 46)
+ROOM = (50, 32, 32)
 SMALL = pl.CostEstimate(flops=1, bytes_accessed=1, transcendentals=0)
 PARAMS = pltpu.CompilerParams(vmem_limit_bytes=32 * 2**20)
 
@@ -71,34 +71,41 @@
     ).astype(jnp.bfloat16)
 
 
-def gradient_kernel(share, along_y_first, waits, me_ref, hidden_ref, upstream_ref, *refs):
-    if waits:
-        refs = refs[waits:]
-    keep_ref, send_ref, place, arrived = refs
+def gradient_kernel(share, along_y_first, waits, streamed, me_ref, hidden_ref, upstream_ref, *refs):
+    refs = refs[waits:]
+    keep_ref, send_ref = refs[:2]
     rows = 2 * SHARE * len(share)
     width = len(share) * BLOCK
+
+    def column(step, owner, block):
+        return pl.multiple_of(((step * 2 + owner) * LAYER + share[block]) * BLOCK, BLOCK)
 
     def copies(step):
         found = []
         for owner in range(2):
-            start = (step * 2 + owner) * LAYER * BLOCK + share[0] * BLOCK
-            source = upstream_ref.at[:, pl.ds(pl.multiple_of(start, BLOCK), width)]
+            place, arrived = refs[2:]
+            source = upstream_ref.at[:, pl.ds(column(step, owner, 0), width)]
             found.append(pltpu.make_async_copy(source, place.at[step, owner], arrived.at[step, owner]))
         return found
 
-    for step in range(STEPS):
-        for copy in copies(step):
-            copy.start()
+    if streamed:
+        for step in range(STEPS):
+            for copy in copies(step):
+                copy.start()
     left = ordered(hidden_ref[...], me_ref[0], along_y_first)
 
     def one_step(step, carry):
-        for copy in copies(step):
-            copy.wait()
+        if streamed:
+            for copy in copies(step):
+                copy.wait()
         blocks = [(owner, block) for owner in range(2) for block in range(len(share))]
         for pair in range(len(share)):
             both = []
             for owner, block in blocks[2 * pair : 2 * pair + 2]:
-                upstream = place[step, owner, :, block * BLOCK : (block + 1) * BLOCK]
+                if streamed:
+                    upstream = refs[2][step, owner, :, block * BLOCK : (block + 1) * BLOCK]
+                else:
+                    upstream = upstream_ref[:, pl.ds(column(step, owner, block), BLOCK)]
                 grad = jnp.dot(left, upstream, preferred_element_type=jnp.float32)
                 both.append(round_to_step(grad).reshape(16, SHARE, BLOCK))
             both = jnp.concatenate(both, axis=1).astype(jnp.bfloat16)
@@ -110,23 +117,24 @@
     lax.fori_loop(0, STEPS, one_step, 0)
 
 
-def gradients(me, hidden, upstream, share, along_y_first, room, after=()):
+def gradients(me, hidden, upstream, share, along_y_first, room, streamed, after=()):
     tokens = upstream.shape[0]
     out = jax.ShapeDtypeStruct((8, OWNERS * len(share) * SHARE, BLOCK), jnp.bfloat16)
+    scratch = [
+        pltpu.VMEM((STEPS, 2, tokens, len(share) * BLOCK), jnp.bfloat16),
+        pltpu.SemaphoreType.DMA((STEPS, 2)),
+    ]
     return pl.pallas_call(
-        functools.partial(gradient_kernel, share, along_y_first, len(after)),
+        functools.partial(gradient_kernel, share, along_y_first, len(after), streamed),
         in_specs=[
             pl.BlockSpec(memory_space=pltpu.SMEM),
             pl.BlockSpec(memory_space=pltpu.VMEM),
-            pl.BlockSpec(memory_space=pltpu.HBM),
+            pl.BlockSpec(memory_space=pltpu.HBM if streamed else pltpu.VMEM),
         ]
         + [pl.BlockSpec(memory_space=pl.ANY)] * len(after),
         out_specs=[pl.BlockSpec(memory_space=pltpu.VMEM)] * 2,
         out_shape=[out, out],
-        scratch_shapes=[
-            pltpu.VMEM((STEPS, 2, tokens, len(share) * BLOCK), jnp.bfloat16),
-            pltpu.SemaphoreType.DMA((STEPS, 2)),
-        ],
+        scratch_shapes=scratch if streamed else [],
         compiler_params=pltpu.CompilerParams(vmem_limit_bytes=room * 2**20),
         cost_estimate=SMALL,
     )(me, hidden, upstream, *after)
@@ -266,14 +274,14 @@
         rows = array.size // BLOCK // parts // 2
         return array.reshape(parts, 2, rows, BLOCK)
 
-    keep_b, go_b = gradients(me, hidden_two, upstream_two, tuple(range(LAYER)), False, ROOM[0])
+    keep_b, go_b = gradients(me, hidden_two, upstream_two, tuple(range(LAYER)), False, ROOM[0], True)
     core_b = send(go_b, TO_CORE)
-    keep_a, go_a = gradients(me, hidden_one, upstream_one, tuple(range(FIRST)), True, ROOM[1])
+    keep_a, go_a = gradients(me, hidden_one, upstream_one, tuple(range(FIRST)), True, ROOM[1], False)
     core_a = send(go_a, TO_CORE)
     b = start_x(halved(keep_b, 4), halved(core_b, 4))
     stay_a, go_a = pair(keep_a, core_a, (b[0],))
     y_a = send(go_a, TO_Y)
-    keep_c, go_c = gradients(me, hidden_one, upstream_one, tuple(range(FIRST, LAYER)), True, ROOM[2], (stay_a,))
+    keep_c, go_c = gradients(me, hidden_one, upstream_one, tuple(range(FIRST, LAYER)), True, ROOM[2], False, (stay_a,))
     core_c = send(go_c, TO_CORE)
     stay_c, go_c = pair(keep_c, core_c)
     y_c = send(go_c, TO_Y)

time: 91.1 us -> 90.6 us (level)
  transfers between devices with their start and end apart: 15 -> 15, of which waited for: 10 -> 10; matrix products, arithmetic and copies ran while one was open for 0% -> 0% of each run, Pallas kernels for 9% -> 8%
where the time goes in v2:
time: 90.6 us; the launch traced here: 90.4 us
  waiting for transfers between devices  33.6 us (37%)
  blocking collectives  22.3 us (25%)
  starting transfers between devices  17.1 us (19%)
  Pallas kernels  15.8 us (17%)
    ppermute x15, waiting for transfers between devices, send(): return lax.ppermute(array, 'intra', pairs)  33.6 us
    all_to_all x1, blocking collectives, body(): lax.all_to_all(node, 'inter', split_axis=0, concat_axis=0, tiled=True)  22.3 us
    ppermute x15, starting transfers between devices, send(): return lax.ppermute(array, 'intra', pairs)  17.1 us
    pallas_call x3, Pallas kernels, gradients(): pl.pallas_call(functools.partial(gradient_kernel, share, along_y_first, l...  12.7 us
  transfers between devices with their start and end apart: 15, of which 10 were waited for; matrix products, arithmetic and copies ran while one was open for 0% of the time, Pallas kernels for 8%

profile of v2, /device:TPU:32, one launch (start us, length us, event | category | flops | bytes accessed | tf_op | source)
XLA Modules:
  0.0 90.4 jit_solution(3872541190295475062)
XLA Ops:
  0.6 0.0 copy-start.2
  0.6 0.7 copy-done.2
  1.4 0.0 copy-start.1
  1.4 5.9 %shard_map.60 = (bf16[8,768,128]{2,1,0:T(8,128)(2,1)S(1)}, bf16[8,768,128]{2,1,0:T(8,128)(2,1)S(1)}) custom-call(s32[1]{0:T(128)} %bitcast.me_ref, bf16[128,128]{1,0:T(8,128)(2,1)S(1)} %copy-done.2, bf16[128,12288]{1,0:T(8,128)(2,1)} %upstream_ref.4), custom_call_target="tpu_custom_call" | custom-call | flops 1 | bytes 1 | tf_op jit(solution)/shard_map/pallas_call | solution.py:127
  7.3 0.1 collective-permute-start.1
  7.4 0.0 copy-done
  7.4 0.0 copy-done.1
  7.4 3.9 %shard_map.59 = (bf16[8,512,128]{2,1,0:T(8,128)(2,1)S(1)}, bf16[8,512,128]{2,1,0:T(8,128)(2,1)S(1)}) custom-call(s32[1]{0:T(128)} %bitcast.me_ref, bf16[128,128]{1,0:T(8,128)(2,1)S(1)} %copy-done.1, bf16[128,12288]{1,0:T(8,128)(2,1)S(1)} %copy-done), custom_call_target="tpu_custom_call" | custom-call | flops 1 | bytes 1 | tf_op jit(solution)/shard_map/pallas_call | solution.py:127
  11.3 0.6 collective-permute-start
  11.9 0.0 collective-permute-done.1
  11.9 0.3 shard_map.61
  12.2 2.0 %collective-permute-done.refs_1_ = bf16[8,512,128]{2,1,0:T(8,128)(2,1)S(1)} collective-permute-done((bf16[8,512,128]{2,1,0:T(8,128)(2,1)S(1)}, bf16[8,512,128]{2,1,0:T(8,128)(2,1)S(1)}, u32[]{:S(2)}, u32[]{:S(2)}) %collective-permute-start) | collective-permute-done | bytes 1048608 | tf_op jit(solution)/shard_map/ppermute | solution.py:41
  14.2 0.2 shard_map.62
  14.4 1.7 %collective-permute-start.2 = (f32[4,512,128]{2,1,0:T(8,128)S(1)}, f32[4,512,128]{2,1,0:T(8,128)S(1)}, u32[]{:S(2)}, u32[]{:S(2)}) collective-permute-start(f32[4,512,128]{2,1,0:T(8,128)S(1)} %get-tuple-element.36), channel_id=1, source_target_pairs={{0,32},{16,48},{32,0},{48,16},{64,96},{80,112},{96,64},{112,80},{1... | collective-permute-start | bytes 3145736 | tf_op jit(solution)/shard_map/ppermute | solution.py:41
  16.1 1.5 %collective-permute-start.3 = (f32[2,768,128]{2,1,0:T(8,128)S(1)}, f32[2,768,128]{2,1,0:T(8,128)S(1)}, u32[]{:S(2)}, u32[]{:S(2)}) collective-permute-start(f32[2,768,128]{2,1,0:T(8,128)S(1)} %get-tuple-element.39), channel_id=1, source_target_pairs={{0,64},{16,80},{32,96},{48,112},{64,0},{80,16},{96,32},{112,48},{1... | collective-permute-start | bytes 2359304 | tf_op jit(solution)/shard_map/ppermute | solution.py:41
  17.6 2.1 %collective-permute-start.4 = (f32[2,768,128]{2,1,0:T(8,128)S(1)}, f32[2,768,128]{2,1,0:T(8,128)S(1)}, u32[]{:S(2)}, u32[]{:S(2)}) collective-permute-start(f32[2,768,128]{2,1,0:T(8,128)S(1)} %get-tuple-element.40), channel_id=1, source_target_pairs={{0,192},{16,208},{32,224},{48,240},{64,128},{80,144},{96,160},{112... | collective-permute-start | bytes 2359304 | tf_op jit(solution)/shard_map/ppermute | solution.py:41
  19.7 2.9 %shard_map.63 = (bf16[8,256,128]{2,1,0:T(8,128)(2,1)S(1)}, bf16[8,256,128]{2,1,0:T(8,128)(2,1)S(1)}) custom-call(s32[1]{0:T(128)} %bitcast.me_ref, bf16[128,128]{1,0:T(8,128)(2,1)S(1)} %copy-done.1, bf16[128,12288]{1,0:T(8,128)(2,1)S(1)} %copy-done, f32[4,512,128]{2,1,0:T(8,128)S(1)} %get-tuple-element.35.refs_0_), custom_call_target="tpu_custom_call" | custom-call | flops 1 | bytes 1 | tf_op jit(solution)/shard_map/pallas_call | solution.py:127
  22.6 0.1 collective-permute-start.5
  22.7 1.9 %collective-permute-done.5.refs_1_ = bf16[8,256,128]{2,1,0:T(8,128)(2,1)S(1)} collective-permute-done((bf16[8,256,128]{2,1,0:T(8,128)(2,1)S(1)}, bf16[8,256,128]{2,1,0:T(8,128)(2,1)S(1)}, u32[]{:S(2)}, u32[]{:S(2)}) %collective-permute-start.5) | collective-permute-done | bytes 524320 | tf_op jit(solution)/shard_map/ppermute | solution.py:41
  24.6 0.1 shard_map.64
  24.7 0.5 collective-permute-start.8
  25.2 10.4 %collective-permute-done.3.refs_2_.refs_1_ = f32[2,768,128]{2,1,0:T(8,128)S(1)} collective-permute-done((f32[2,768,128]{2,1,0:T(8,128)S(1)}, f32[2,768,128]{2,1,0:T(8,128)S(1)}, u32[]{:S(2)}, u32[]{:S(2)}) %collective-permute-start.3) | collective-permute-done | bytes 786464 | tf_op jit(solution)/shard_map/ppermute | solution.py:41
  35.6 2.4 %collective-permute-done.4.refs_3_.refs_2_ = f32[2,768,128]{2,1,0:T(8,128)S(1)} collective-permute-done((f32[2,768,128]{2,1,0:T(8,128)S(1)}, f32[2,768,128]{2,1,0:T(8,128)S(1)}, u32[]{:S(2)}, u32[]{:S(2)}) %collective-permute-start.4) | collective-permute-done | bytes 786464 | tf_op jit(solution)/shard_map/ppermute | solution.py:41
  38.0 0.1 shard_map.65
  38.1 2.2 %collective-permute-start.10 = (f32[768,128]{1,0:T(8,128)S(1)}, f32[768,128]{1,0:T(8,128)S(1)}, u32[]{:S(2)}, u32[]{:S(2)}) collective-permute-start(f32[768,128]{1,0:T(8,128)S(1)} %get-tuple-element.45.refs_3_), channel_id=1, source_target_pairs={{0,192},{16,208},{32,224},{48,240},{64,128},{80,144},{96,160},{112... | collective-permute-start | bytes 1179656 | tf_op jit(solution)/shard_map/ppermute | solution.py:41
  40.3 0.0 collective-permute-start.9
  40.3 0.2 collective-permute-done.2
  40.5 0.1 shard_map.66
  40.6 1.9 %collective-permute-start.6 = (f32[2,256,128]{2,1,0:T(8,128)S(1)}, f32[2,256,128]{2,1,0:T(8,128)S(1)}, u32[]{:S(2)}, u32[]{:S(2)}) collective-permute-start(f32[2,256,128]{2,1,0:T(8,128)S(1)} %get-tuple-element.47), channel_id=1, source_target_pairs={{0,64},{16,80},{32,96},{48,112},{64,0},{80,16},{96,32},{112,48},{1... | collective-permute-start | bytes 786440 | tf_op jit(solution)/shard_map/ppermute | solution.py:41
  42.6 1.7 %collective-permute-start.7 = (f32[2,256,128]{2,1,0:T(8,128)S(1)}, f32[2,256,128]{2,1,0:T(8,128)S(1)}, u32[]{:S(2)}, u32[]{:S(2)}) collective-permute-start(f32[2,256,128]{2,1,0:T(8,128)S(1)} %get-tuple-element.48), channel_id=1, source_target_pairs={{0,192},{16,208},{32,224},{48,240},{64,128},{80,144},{96,160},{112... | collective-permute-start | bytes 786440 | tf_op jit(solution)/shard_map/ppermute | solution.py:41
  44.3 7.2 %collective-permute-done.10.refs_4_ = f32[768,128]{1,0:T(8,128)S(1)} collective-permute-done((f32[768,128]{1,0:T(8,128)S(1)}, f32[768,128]{1,0:T(8,128)S(1)}, u32[]{:S(2)}, u32[]{:S(2)}) %collective-permute-start.10) | collective-permute-done | bytes 393248 | tf_op jit(solution)/shard_map/ppermute | solution.py:41
  51.5 0.9 collective-permute-done.9.refs_3_
  52.4 0.1 shard_map.67
  52.5 0.5 collective-permute-start.14
  53.0 0.0 collective-permute-done.8.refs_1_
  53.0 2.6 %collective-permute-done.6.refs_4_.refs_1_ = f32[2,256,128]{2,1,0:T(8,128)S(1)} collective-permute-done((f32[2,256,128]{2,1,0:T(8,128)S(1)}, f32[2,256,128]{2,1,0:T(8,128)S(1)}, u32[]{:S(2)}, u32[]{:S(2)}) %collective-permute-start.6) | collective-permute-done | bytes 262176 | tf_op jit(solution)/shard_map/ppermute | solution.py:41
  55.6 0.0 collective-permute-done.7.refs_5_.refs_2_
  55.6 0.1 shard_map.68
  55.7 0.4 collective-permute-start.11
  56.0 1.3 %collective-permute-start.12 = (f32[512,128]{1,0:T(8,128)S(1)}, f32[512,128]{1,0:T(8,128)S(1)}, u32[]{:S(2)}, u32[]{:S(2)}) collective-permute-start(f32[512,128]{1,0:T(8,128)S(1)} %get-tuple-element.55), channel_id=1, source_target_pairs={{0,192},{16,208},{32,224},{48,240},{64,128},{80,144},{96,160},{112... | collective-permute-start | bytes 786440 | tf_op jit(solution)/shard_map/ppermute | solution.py:41
  57.4 2.5 %collective-permute-start.13 = (f32[256,128]{1,0:T(8,128)S(1)}, f32[256,128]{1,0:T(8,128)S(1)}, u32[]{:S(2)}, u32[]{:S(2)}) collective-permute-start(f32[256,128]{1,0:T(8,128)S(1)} %get-tuple-element.56), channel_id=1, source_target_pairs={{0,128},{16,144},{32,160},{48,176},{64,192},{80,208},{96,224},{112... | collective-permute-start | bytes 393224 | tf_op jit(solution)/shard_map/ppermute | solution.py:41
  59.9 6.0 %collective-permute-done.13.refs_6_ = f32[256,128]{1,0:T(8,128)S(1)} collective-permute-done((f32[256,128]{1,0:T(8,128)S(1)}, f32[256,128]{1,0:T(8,128)S(1)}, u32[]{:S(2)}, u32[]{:S(2)}) %collective-permute-start.13) | collective-permute-done | bytes 131104 | tf_op jit(solution)/shard_map/ppermute | solution.py:41
  65.8 0.0 collective-permute-done.11.refs_4_
  65.8 0.2 collective-permute-done.12.refs_5_
  66.0 0.0 collective-permute-done.14.refs_8_
  66.0 0.4 shard_map.69
  66.4 22.3 %all_to_all.5.pieces_ref = bf16[16,96,128]{2,1,0:T(8,128)(2,1)} all-to-all(bf16[16,96,128]{2,1,0:T(8,128)(2,1)S(1)} %shard_map.69), channel_id=1, replica_groups=mesh['intra'=16,'inter'=16] {'inter'}, dimensions={0} | all-to-all | bytes 786432 | tf_op jit(solution)/shard_map/all_to_all | solution.py:311
  88.7 1.7 %shard_map.70 = (f32[8,768]{1,0:T(8,128)}, f32[8,768]{1,0:T(8,128)}) custom-call(bf16[16,96,128]{2,1,0:T(8,128)(2,1)} %all_to_all.5.pieces_ref), custom_call_target="tpu_custom_call" | custom-call | tf_op jit(solution)/shard_map/pallas_call | solution.py:314
  (1 shorter events, 0.0 us)
Async XLA Ops:
  0.6 0.8 copy-start.2
  1.4 6.0 %copy-start = (bf16[128,12288]{1,0:T(8,128)(2,1)S(1)}, bf16[128,12288]{1,0:T(8,128)(2,1)}, u32[]{:S(2)}) copy-start(bf16[128,12288]{1,0:T(8,128)(2,1)} %upstream_ref.5) | copy-start | bytes 9437188
  1.4 6.0 %copy-start.1 = (bf16[128,128]{1,0:T(8,128)(2,1)S(1)}, bf16[128,128]{1,0:T(8,128)(2,1)}, u32[]{:S(2)}) copy-start(bf16[128,128]{1,0:T(8,128)(2,1)} %hidden_ref.5) | copy-start | bytes 98308
  7.3 4.6 %collective-permute-start.1 = (bf16[8,768,128]{2,1,0:T(8,128)(2,1)S(1)}, bf16[8,768,128]{2,1,0:T(8,128)(2,1)S(1)}, u32[]{:S(2)}, u32[]{:S(2)}) collective-permute-start(bf16[8,768,128]{2,1,0:T(8,128)(2,1)S(1)} %get-tuple-element.33), channel_id=1, source_target_pairs={{0,16},{16,0},{32,48},{48,32},{64,80},{80,64},{96,112},{112,96},{1... | collective-permute-start | bytes 4718600 | tf_op jit(solution)/shard_map/ppermute | solution.py:41
  11.3 2.9 %collective-permute-start = (bf16[8,512,128]{2,1,0:T(8,128)(2,1)S(1)}, bf16[8,512,128]{2,1,0:T(8,128)(2,1)S(1)}, u32[]{:S(2)}, u32[]{:S(2)}) collective-permute-start(bf16[8,512,128]{2,1,0:T(8,128)(2,1)S(1)} %get-tuple-element.31), channel_id=1, source_target_pairs={{0,16},{16,0},{32,48},{48,32},{64,80},{80,64},{96,112},{112,96},{1... | collective-permute-start | bytes 3145736 | tf_op jit(solution)/shard_map/ppermute | solution.py:41
  14.4 26.1 %collective-permute-start.2 = (f32[4,512,128]{2,1,0:T(8,128)S(1)}, f32[4,512,128]{2,1,0:T(8,128)S(1)}, u32[]{:S(2)}, u32[]{:S(2)}) collective-permute-start(f32[4,512,128]{2,1,0:T(8,128)S(1)} %get-tuple-element.36), channel_id=1, source_target_pairs={{0,32},{16,48},{32,0},{48,16},{64,96},{80,112},{96,64},{112,80},{1... | collective-permute-start | bytes 3145736 | tf_op jit(solution)/shard_map/ppermute | solution.py:41
  16.1 19.5 %collective-permute-start.3 = (f32[2,768,128]{2,1,0:T(8,128)S(1)}, f32[2,768,128]{2,1,0:T(8,128)S(1)}, u32[]{:S(2)}, u32[]{:S(2)}) collective-permute-start(f32[2,768,128]{2,1,0:T(8,128)S(1)} %get-tuple-element.39), channel_id=1, source_target_pairs={{0,64},{16,80},{32,96},{48,112},{64,0},{80,16},{96,32},{112,48},{1... | collective-permute-start | bytes 2359304 | tf_op jit(solution)/shard_map/ppermute | solution.py:41
  17.6 20.5 %collective-permute-start.4 = (f32[2,768,128]{2,1,0:T(8,128)S(1)}, f32[2,768,128]{2,1,0:T(8,128)S(1)}, u32[]{:S(2)}, u32[]{:S(2)}) collective-permute-start(f32[2,768,128]{2,1,0:T(8,128)S(1)} %get-tuple-element.40), channel_id=1, source_target_pairs={{0,192},{16,208},{32,224},{48,240},{64,128},{80,144},{96,160},{112... | collective-permute-start | bytes 2359304 | tf_op jit(solution)/shard_map/ppermute | solution.py:41
  22.6 2.0 %collective-permute-start.5 = (bf16[8,256,128]{2,1,0:T(8,128)(2,1)S(1)}, bf16[8,256,128]{2,1,0:T(8,128)(2,1)S(1)}, u32[]{:S(2)}, u32[]{:S(2)}) collective-permute-start(bf16[8,256,128]{2,1,0:T(8,128)(2,1)S(1)} %get-tuple-element.42), channel_id=1, source_target_pairs={{0,16},{16,0},{32,48},{48,32},{64,80},{80,64},{96,112},{112,96},{1... | collective-permute-start | bytes 1572872 | tf_op jit(solution)/shard_map/ppermute | solution.py:41
  24.7 28.3 %collective-permute-start.8 = (f32[4,256,128]{2,1,0:T(8,128)S(1)}, f32[4,256,128]{2,1,0:T(8,128)S(1)}, u32[]{:S(2)}, u32[]{:S(2)}) collective-permute-start(f32[4,256,128]{2,1,0:T(8,128)S(1)} %get-tuple-element.43.refs_4_), channel_id=1, source_target_pairs={{0,32},{16,48},{32,0},{48,16},{64,96},{80,112},{96,64},{112,80},{1... | collective-permute-start | bytes 1572872 | tf_op jit(solution)/shard_map/ppermute | solution.py:41
  38.1 13.3 %collective-permute-start.10 = (f32[768,128]{1,0:T(8,128)S(1)}, f32[768,128]{1,0:T(8,128)S(1)}, u32[]{:S(2)}, u32[]{:S(2)}) collective-permute-start(f32[768,128]{1,0:T(8,128)S(1)} %get-tuple-element.45.refs_3_), channel_id=1, source_target_pairs={{0,192},{16,208},{32,224},{48,240},{64,128},{80,144},{96,160},{112... | collective-permute-start | bytes 1179656 | tf_op jit(solution)/shard_map/ppermute | solution.py:41
  40.3 12.1 %collective-permute-start.9 = (f32[768,128]{1,0:T(8,128)S(1)}, f32[768,128]{1,0:T(8,128)S(1)}, u32[]{:S(2)}, u32[]{:S(2)}) collective-permute-start(f32[768,128]{1,0:T(8,128)S(1)} %get-tuple-element.44.refs_2_), channel_id=1, source_target_pairs={{0,64},{16,80},{32,96},{48,112},{64,0},{80,16},{96,32},{112,48},{1... | collective-permute-start | bytes 1179656 | tf_op jit(solution)/shard_map/ppermute | solution.py:41
  40.6 15.0 %collective-permute-start.6 = (f32[2,256,128]{2,1,0:T(8,128)S(1)}, f32[2,256,128]{2,1,0:T(8,128)S(1)}, u32[]{:S(2)}, u32[]{:S(2)}) collective-permute-start(f32[2,256,128]{2,1,0:T(8,128)S(1)} %get-tuple-element.47), channel_id=1, source_target_pairs={{0,64},{16,80},{32,96},{48,112},{64,0},{80,16},{96,32},{112,48},{1... | collective-permute-start | bytes 786440 | tf_op jit(solution)/shard_map/ppermute | solution.py:41
  42.6 13.0 %collective-permute-start.7 = (f32[2,256,128]{2,1,0:T(8,128)S(1)}, f32[2,256,128]{2,1,0:T(8,128)S(1)}, u32[]{:S(2)}, u32[]{:S(2)}) collective-permute-start(f32[2,256,128]{2,1,0:T(8,128)S(1)} %get-tuple-element.48), channel_id=1, source_target_pairs={{0,192},{16,208},{32,224},{48,240},{64,128},{80,144},{96,160},{112... | collective-permute-start | bytes 786440 | tf_op jit(solution)/shard_map/ppermute | solution.py:41
  52.5 13.5 %collective-permute-start.14 = (f32[768,128]{1,0:T(8,128)S(1)}, f32[768,128]{1,0:T(8,128)S(1)}, u32[]{:S(2)}, u32[]{:S(2)}) collective-permute-start(f32[768,128]{1,0:T(8,128)S(1)} %get-tuple-element.52.refs_6_), channel_id=1, source_target_pairs={{0,32},{16,48},{32,0},{48,16},{64,96},{80,112},{96,64},{112,80},{1... | collective-permute-start | bytes 1179656 | tf_op jit(solution)/shard_map/ppermute | solution.py:41
  55.7 10.1 %collective-permute-start.11 = (f32[512,128]{1,0:T(8,128)S(1)}, f32[512,128]{1,0:T(8,128)S(1)}, u32[]{:S(2)}, u32[]{:S(2)}) collective-permute-start(f32[512,128]{1,0:T(8,128)S(1)} %get-tuple-element.54), channel_id=1, source_target_pairs={{0,64},{16,80},{32,96},{48,112},{64,0},{80,16},{96,32},{112,48},{1... | collective-permute-start | bytes 786440 | tf_op jit(solution)/shard_map/ppermute | solution.py:41
  56.0 9.9 %collective-permute-start.12 = (f32[512,128]{1,0:T(8,128)S(1)}, f32[512,128]{1,0:T(8,128)S(1)}, u32[]{:S(2)}, u32[]{:S(2)}) collective-permute-start(f32[512,128]{1,0:T(8,128)S(1)} %get-tuple-element.55), channel_id=1, source_target_pairs={{0,192},{16,208},{32,224},{48,240},{64,128},{80,144},{96,160},{112... | collective-permute-start | bytes 786440 | tf_op jit(solution)/shard_map/ppermute | solution.py:41
  57.4 8.5 %collective-permute-start.13 = (f32[256,128]{1,0:T(8,128)S(1)}, f32[256,128]{1,0:T(8,128)S(1)}, u32[]{:S(2)}, u32[]{:S(2)}) collective-permute-start(f32[256,128]{1,0:T(8,128)S(1)} %get-tuple-element.56), channel_id=1, source_target_pairs={{0,128},{16,144},{32,160},{48,176},{64,192},{80,208},{96,224},{112... | collective-permute-start | bytes 393224 | tf_op jit(solution)/shard_map/ppermute | solution.py:41

commit v3 on v2

--- a/solution.py
+++ b/solution.py
@@ -13,6 +13,7 @@
 X, Y, CORES = 4, 2, 2
 OWNERS = 16
 STEPS = OWNERS // 2
+WAITS = ((0, 1), (1, 3), (3, STEPS))
 LAYER = 6
 FIRST = 4
 ROOM = (50, 32, 32)
@@ -78,7 +79,8 @@
     width = len(share) * BLOCK
 
     def column(step, owner, block):
-        return pl.multiple_of(((step * 2 + owner) * LAYER + share[block]) * BLOCK, BLOCK)
+        start = ((step * 2 + owner) * LAYER + share[block]) * BLOCK
+        return start if isinstance(start, int) else pl.multiple_of(start, BLOCK)
 
     def copies(step):
         found = []
@@ -95,9 +97,6 @@
     left = ordered(hidden_ref[...], me_ref[0], along_y_first)
 
     def one_step(step, carry):
-        if streamed:
-            for copy in copies(step):
-                copy.wait()
         blocks = [(owner, block) for owner in range(2) for block in range(len(share))]
         for pair in range(len(share)):
             both = []
@@ -109,12 +108,21 @@
                 grad = jnp.dot(left, upstream, preferred_element_type=jnp.float32)
                 both.append(round_to_step(grad).reshape(16, SHARE, BLOCK))
             both = jnp.concatenate(both, axis=1).astype(jnp.bfloat16)
-            at = pl.ds(pl.multiple_of(step * rows + pair * 2 * SHARE, 2 * SHARE), 2 * SHARE)
+            start = step * rows + pair * 2 * SHARE
+            at = pl.ds(start if isinstance(start, int) else pl.multiple_of(start, 2 * SHARE), 2 * SHARE)
             keep_ref[:, at, :] = both[:8]
             send_ref[:, at, :] = both[8:]
         return carry
 
-    lax.fori_loop(0, STEPS, one_step, 0)
+    if streamed:
+        for begin, end in WAITS:
+            for step in range(begin, end):
+                for copy in copies(step):
+                    copy.wait()
+            for step in range(begin, end):
+                one_step(step, 0)
+    else:
+        lax.fori_loop(0, STEPS, one_step, 0, unroll=4)
 
 
 def gradients(me, hidden, upstream, share, along_y_first, room, streamed, after=()):

time: 90.6 us -> 88.3 us (0.975)
  Pallas kernels: 15.8 us -> 12.3 us
  waiting for transfers between devices: 33.6 us -> 34.9 us
    pallas_call x3, Pallas kernels: 12.7 us -> 9.13 us  [gradients(): pl.pallas_call(functools.partial(gradient_kernel, share, along_y_first, l...]
    ppermute x15, waiting for transfers between devices: 33.6 us -> 34.9 us  [send(): return lax.ppermute(array, 'intra', pairs)]
  transfers between devices with their start and end apart: 15 -> 15, of which waited for: 10 -> 11; matrix products, arithmetic and copies ran while one was open for 0% -> 0% of each run, Pallas kernels for 8% -> 6%
where the time goes in v3:
time: 88.3 us; the launch traced here: 88.1 us
  waiting for transfers between devices  34.9 us (40%)
  blocking collectives  22.3 us (25%)
  starting transfers between devices  17.1 us (19%)
  Pallas kernels  12.3 us (14%)
    ppermute x15, waiting for transfers between devices, send(): return lax.ppermute(array, 'intra', pairs)  34.9 us
    all_to_all x1, blocking collectives, body(): lax.all_to_all(node, 'inter', split_axis=0, concat_axis=0, tiled=True)  22.3 us
    ppermute x15, starting transfers between devices, send(): return lax.ppermute(array, 'intra', pairs)  17.1 us
    pallas_call x3, Pallas kernels, gradients(): pl.pallas_call(functools.partial(gradient_kernel, share, along_y_first, l...  9.13 us
  transfers between devices with their start and end apart: 15, of which 11 were waited for; matrix products, arithmetic and copies ran while one was open for 0% of the time, Pallas kernels for 6%

profile of v3, /device:TPU:32, one launch (start us, length us, event | category | flops | bytes accessed | tf_op | source)
XLA Modules:
  0.0 88.1 jit_solution(17566630728443712339)
XLA Ops:
  0.6 0.0 copy-start.2
  0.6 0.7 copy-done.2
  1.4 0.0 copy-start
  1.4 4.8 %shard_map.60 = (bf16[8,768,128]{2,1,0:T(8,128)(2,1)S(1)}, bf16[8,768,128]{2,1,0:T(8,128)(2,1)S(1)}) custom-call(s32[1]{0:T(128)} %bitcast.me_ref, bf16[128,128]{1,0:T(8,128)(2,1)S(1)} %copy-done.2, bf16[128,12288]{1,0:T(8,128)(2,1)} %upstream_ref.4), custom_call_target="tpu_custom_call" | custom-call | flops 1 | bytes 1 | tf_op jit(solution)/shard_map/pallas_call | solution.py:135
  6.2 0.1 collective-permute-start.1
  6.3 0.0 copy-done
  6.3 0.0 copy-done.1
  6.3 2.7 %shard_map.59 = (bf16[8,512,128]{2,1,0:T(8,128)(2,1)S(1)}, bf16[8,512,128]{2,1,0:T(8,128)(2,1)S(1)}) custom-call(s32[1]{0:T(128)} %bitcast.me_ref, bf16[128,128]{1,0:T(8,128)(2,1)S(1)} %copy-done.1, bf16[128,12288]{1,0:T(8,128)(2,1)S(1)} %copy-done), custom_call_target="tpu_custom_call" | custom-call | flops 1 | bytes 1 | tf_op jit(solution)/shard_map/pallas_call | solution.py:135
  9.0 0.6 collective-permute-start
  9.6 0.1 collective-permute-done.1
  9.7 0.3 shard_map.61
  10.0 1.8 %collective-permute-done.refs_1_ = bf16[8,512,128]{2,1,0:T(8,128)(2,1)S(1)} collective-permute-done((bf16[8,512,128]{2,1,0:T(8,128)(2,1)S(1)}, bf16[8,512,128]{2,1,0:T(8,128)(2,1)S(1)}, u32[]{:S(2)}, u32[]{:S(2)}) %collective-permute-start) | collective-permute-done | bytes 1048608 | tf_op jit(solution)/shard_map/ppermute | solution.py:42
  11.9 0.2 shard_map.62
  12.1 1.7 %collective-permute-start.2 = (f32[4,512,128]{2,1,0:T(8,128)S(1)}, f32[4,512,128]{2,1,0:T(8,128)S(1)}, u32[]{:S(2)}, u32[]{:S(2)}) collective-permute-start(f32[4,512,128]{2,1,0:T(8,128)S(1)} %get-tuple-element.36), channel_id=1, source_target_pairs={{0,32},{16,48},{32,0},{48,16},{64,96},{80,112},{96,64},{112,80},{1... | collective-permute-start | bytes 3145736 | tf_op jit(solution)/shard_map/ppermute | solution.py:42
  13.8 1.5 %collective-permute-start.3 = (f32[2,768,128]{2,1,0:T(8,128)S(1)}, f32[2,768,128]{2,1,0:T(8,128)S(1)}, u32[]{:S(2)}, u32[]{:S(2)}) collective-permute-start(f32[2,768,128]{2,1,0:T(8,128)S(1)} %get-tuple-element.39), channel_id=1, source_target_pairs={{0,64},{16,80},{32,96},{48,112},{64,0},{80,16},{96,32},{112,48},{1... | collective-permute-start | bytes 2359304 | tf_op jit(solution)/shard_map/ppermute | solution.py:42
  15.3 2.1 %collective-permute-start.4 = (f32[2,768,128]{2,1,0:T(8,128)S(1)}, f32[2,768,128]{2,1,0:T(8,128)S(1)}, u32[]{:S(2)}, u32[]{:S(2)}) collective-permute-start(f32[2,768,128]{2,1,0:T(8,128)S(1)} %get-tuple-element.40), channel_id=1, source_target_pairs={{0,192},{16,208},{32,224},{48,240},{64,128},{80,144},{96,160},{112... | collective-permute-start | bytes 2359304 | tf_op jit(solution)/shard_map/ppermute | solution.py:42
  17.4 1.6 %shard_map.63 = (bf16[8,256,128]{2,1,0:T(8,128)(2,1)S(1)}, bf16[8,256,128]{2,1,0:T(8,128)(2,1)S(1)}) custom-call(s32[1]{0:T(128)} %bitcast.me_ref, bf16[128,128]{1,0:T(8,128)(2,1)S(1)} %copy-done.1, bf16[128,12288]{1,0:T(8,128)(2,1)S(1)} %copy-done, f32[4,512,128]{2,1,0:T(8,128)S(1)} %get-tuple-element.35.refs_0_), custom_call_target="tpu_custom_call" | custom-call | flops 1 | bytes 1 | tf_op jit(solution)/shard_map/pallas_call | solution.py:135
  19.0 0.1 collective-permute-start.5
  19.1 1.9 %collective-permute-done.5.refs_1_ = bf16[8,256,128]{2,1,0:T(8,128)(2,1)S(1)} collective-permute-done((bf16[8,256,128]{2,1,0:T(8,128)(2,1)S(1)}, bf16[8,256,128]{2,1,0:T(8,128)(2,1)S(1)}, u32[]{:S(2)}, u32[]{:S(2)}) %collective-permute-start.5) | collective-permute-done | bytes 524320 | tf_op jit(solution)/shard_map/ppermute | solution.py:42
  21.0 0.1 shard_map.64
  21.1 0.5 collective-permute-start.8
  21.7 11.6 %collective-permute-done.3.refs_2_.refs_1_ = f32[2,768,128]{2,1,0:T(8,128)S(1)} collective-permute-done((f32[2,768,128]{2,1,0:T(8,128)S(1)}, f32[2,768,128]{2,1,0:T(8,128)S(1)}, u32[]{:S(2)}, u32[]{:S(2)}) %collective-permute-start.3) | collective-permute-done | bytes 786464 | tf_op jit(solution)/shard_map/ppermute | solution.py:42
  33.3 2.4 %collective-permute-done.4.refs_3_.refs_2_ = f32[2,768,128]{2,1,0:T(8,128)S(1)} collective-permute-done((f32[2,768,128]{2,1,0:T(8,128)S(1)}, f32[2,768,128]{2,1,0:T(8,128)S(1)}, u32[]{:S(2)}, u32[]{:S(2)}) %collective-permute-start.4) | collective-permute-done | bytes 786464 | tf_op jit(solution)/shard_map/ppermute | solution.py:42
  35.7 0.1 shard_map.65
  35.8 2.2 %collective-permute-start.10 = (f32[768,128]{1,0:T(8,128)S(1)}, f32[768,128]{1,0:T(8,128)S(1)}, u32[]{:S(2)}, u32[]{:S(2)}) collective-permute-start(f32[768,128]{1,0:T(8,128)S(1)} %get-tuple-element.45.refs_3_), channel_id=1, source_target_pairs={{0,192},{16,208},{32,224},{48,240},{64,128},{80,144},{96,160},{112... | collective-permute-start | bytes 1179656 | tf_op jit(solution)/shard_map/ppermute | solution.py:42
  38.0 0.0 collective-permute-start.9
  38.0 0.2 collective-permute-done.2
  38.2 0.1 shard_map.66
  38.3 1.9 %collective-permute-start.6 = (f32[2,256,128]{2,1,0:T(8,128)S(1)}, f32[2,256,128]{2,1,0:T(8,128)S(1)}, u32[]{:S(2)}, u32[]{:S(2)}) collective-permute-start(f32[2,256,128]{2,1,0:T(8,128)S(1)} %get-tuple-element.47), channel_id=1, source_target_pairs={{0,64},{16,80},{32,96},{48,112},{64,0},{80,16},{96,32},{112,48},{1... | collective-permute-start | bytes 786440 | tf_op jit(solution)/shard_map/ppermute | solution.py:42
  40.2 1.7 %collective-permute-start.7 = (f32[2,256,128]{2,1,0:T(8,128)S(1)}, f32[2,256,128]{2,1,0:T(8,128)S(1)}, u32[]{:S(2)}, u32[]{:S(2)}) collective-permute-start(f32[2,256,128]{2,1,0:T(8,128)S(1)} %get-tuple-element.48), channel_id=1, source_target_pairs={{0,192},{16,208},{32,224},{48,240},{64,128},{80,144},{96,160},{112... | collective-permute-start | bytes 786440 | tf_op jit(solution)/shard_map/ppermute | solution.py:42
  42.0 7.2 %collective-permute-done.10.refs_4_ = f32[768,128]{1,0:T(8,128)S(1)} collective-permute-done((f32[768,128]{1,0:T(8,128)S(1)}, f32[768,128]{1,0:T(8,128)S(1)}, u32[]{:S(2)}, u32[]{:S(2)}) %collective-permute-start.10) | collective-permute-done | bytes 393248 | tf_op jit(solution)/shard_map/ppermute | solution.py:42
  49.2 0.9 collective-permute-done.9.refs_3_
  50.1 0.1 shard_map.67
  50.2 0.6 collective-permute-start.14
  50.7 0.0 collective-permute-done.8.refs_1_
  50.7 2.5 %collective-permute-done.6.refs_4_.refs_1_ = f32[2,256,128]{2,1,0:T(8,128)S(1)} collective-permute-done((f32[2,256,128]{2,1,0:T(8,128)S(1)}, f32[2,256,128]{2,1,0:T(8,128)S(1)}, u32[]{:S(2)}, u32[]{:S(2)}) %collective-permute-start.6) | collective-permute-done | bytes 262176 | tf_op jit(solution)/shard_map/ppermute | solution.py:42
  53.3 0.0 collective-permute-done.7.refs_5_.refs_2_
  53.3 0.1 shard_map.68
  53.4 0.4 collective-permute-start.11
  53.7 1.3 %collective-permute-start.12 = (f32[512,128]{1,0:T(8,128)S(1)}, f32[512,128]{1,0:T(8,128)S(1)}, u32[]{:S(2)}, u32[]{:S(2)}) collective-permute-start(f32[512,128]{1,0:T(8,128)S(1)} %get-tuple-element.55), channel_id=1, source_target_pairs={{0,192},{16,208},{32,224},{48,240},{64,128},{80,144},{96,160},{112... | collective-permute-start | bytes 786440 | tf_op jit(solution)/shard_map/ppermute | solution.py:42
  55.0 2.5 %collective-permute-start.13 = (f32[256,128]{1,0:T(8,128)S(1)}, f32[256,128]{1,0:T(8,128)S(1)}, u32[]{:S(2)}, u32[]{:S(2)}) collective-permute-start(f32[256,128]{1,0:T(8,128)S(1)} %get-tuple-element.56), channel_id=1, source_target_pairs={{0,128},{16,144},{32,160},{48,176},{64,192},{80,208},{96,224},{112... | collective-permute-start | bytes 393224 | tf_op jit(solution)/shard_map/ppermute | solution.py:42
  57.5 6.0 %collective-permute-done.13.refs_6_ = f32[256,128]{1,0:T(8,128)S(1)} collective-permute-done((f32[256,128]{1,0:T(8,128)S(1)}, f32[256,128]{1,0:T(8,128)S(1)}, u32[]{:S(2)}, u32[]{:S(2)}) %collective-permute-start.13) | collective-permute-done | bytes 131104 | tf_op jit(solution)/shard_map/ppermute | solution.py:42
  63.5 0.0 collective-permute-done.11.refs_4_
  63.5 0.2 collective-permute-done.12.refs_5_
  63.7 0.0 collective-permute-done.14.refs_8_
  63.7 0.4 shard_map.69
  64.1 22.3 %all_to_all.5.pieces_ref = bf16[16,96,128]{2,1,0:T(8,128)(2,1)} all-to-all(bf16[16,96,128]{2,1,0:T(8,128)(2,1)S(1)} %shard_map.69), channel_id=1, replica_groups=mesh['intra'=16,'inter'=16] {'inter'}, dimensions={0} | all-to-all | bytes 786432 | tf_op jit(solution)/shard_map/all_to_all | solution.py:319
  86.5 1.7 %shard_map.70 = (f32[8,768]{1,0:T(8,128)}, f32[8,768]{1,0:T(8,128)}) custom-call(bf16[16,96,128]{2,1,0:T(8,128)(2,1)} %all_to_all.5.pieces_ref), custom_call_target="tpu_custom_call" | custom-call | tf_op jit(solution)/shard_map/pallas_call | solution.py:322
  (1 shorter events, 0.0 us)
Async XLA Ops:
  0.6 0.8 copy-start.2
  1.4 4.9 %copy-start = (bf16[128,12288]{1,0:T(8,128)(2,1)S(1)}, bf16[128,12288]{1,0:T(8,128)(2,1)}, u32[]{:S(2)}) copy-start(bf16[128,12288]{1,0:T(8,128)(2,1)} %upstream_ref.5) | copy-start | bytes 9437188
  1.4 4.9 %copy-start.1 = (bf16[128,128]{1,0:T(8,128)(2,1)S(1)}, bf16[128,128]{1,0:T(8,128)(2,1)}, u32[]{:S(2)}) copy-start(bf16[128,128]{1,0:T(8,128)(2,1)} %hidden_ref.5) | copy-start | bytes 98308
  6.2 3.5 %collective-permute-start.1 = (bf16[8,768,128]{2,1,0:T(8,128)(2,1)S(1)}, bf16[8,768,128]{2,1,0:T(8,128)(2,1)S(1)}, u32[]{:S(2)}, u32[]{:S(2)}) collective-permute-start(bf16[8,768,128]{2,1,0:T(8,128)(2,1)S(1)} %get-tuple-element.33), channel_id=1, source_target_pairs={{0,16},{16,0},{32,48},{48,32},{64,80},{80,64},{96,112},{112,96},{1... | collective-permute-start | bytes 4718600 | tf_op jit(solution)/shard_map/ppermute | solution.py:42
  9.0 2.9 %collective-permute-start = (bf16[8,512,128]{2,1,0:T(8,128)(2,1)S(1)}, bf16[8,512,128]{2,1,0:T(8,128)(2,1)S(1)}, u32[]{:S(2)}, u32[]{:S(2)}) collective-permute-start(bf16[8,512,128]{2,1,0:T(8,128)(2,1)S(1)} %get-tuple-element.31), channel_id=1, source_target_pairs={{0,16},{16,0},{32,48},{48,32},{64,80},{80,64},{96,112},{112,96},{1... | collective-permute-start | bytes 3145736 | tf_op jit(solution)/shard_map/ppermute | solution.py:42
  12.1 26.1 %collective-permute-start.2 = (f32[4,512,128]{2,1,0:T(8,128)S(1)}, f32[4,512,128]{2,1,0:T(8,128)S(1)}, u32[]{:S(2)}, u32[]{:S(2)}) collective-permute-start(f32[4,512,128]{2,1,0:T(8,128)S(1)} %get-tuple-element.36), channel_id=1, source_target_pairs={{0,32},{16,48},{32,0},{48,16},{64,96},{80,112},{96,64},{112,80},{1... | collective-permute-start | bytes 3145736 | tf_op jit(solution)/shard_map/ppermute | solution.py:42
  13.8 19.5 %collective-permute-start.3 = (f32[2,768,128]{2,1,0:T(8,128)S(1)}, f32[2,768,128]{2,1,0:T(8,128)S(1)}, u32[]{:S(2)}, u32[]{:S(2)}) collective-permute-start(f32[2,768,128]{2,1,0:T(8,128)S(1)} %get-tuple-element.39), channel_id=1, source_target_pairs={{0,64},{16,80},{32,96},{48,112},{64,0},{80,16},{96,32},{112,48},{1... | collective-permute-start | bytes 2359304 | tf_op jit(solution)/shard_map/ppermute | solution.py:42
  15.3 20.5 %collective-permute-start.4 = (f32[2,768,128]{2,1,0:T(8,128)S(1)}, f32[2,768,128]{2,1,0:T(8,128)S(1)}, u32[]{:S(2)}, u32[]{:S(2)}) collective-permute-start(f32[2,768,128]{2,1,0:T(8,128)S(1)} %get-tuple-element.40), channel_id=1, source_target_pairs={{0,192},{16,208},{32,224},{48,240},{64,128},{80,144},{96,160},{112... | collective-permute-start | bytes 2359304 | tf_op jit(solution)/shard_map/ppermute | solution.py:42
  19.0 2.0 %collective-permute-start.5 = (bf16[8,256,128]{2,1,0:T(8,128)(2,1)S(1)}, bf16[8,256,128]{2,1,0:T(8,128)(2,1)S(1)}, u32[]{:S(2)}, u32[]{:S(2)}) collective-permute-start(bf16[8,256,128]{2,1,0:T(8,128)(2,1)S(1)} %get-tuple-element.42), channel_id=1, source_target_pairs={{0,16},{16,0},{32,48},{48,32},{64,80},{80,64},{96,112},{112,96},{1... | collective-permute-start | bytes 1572872 | tf_op jit(solution)/shard_map/ppermute | solution.py:42
  21.1 29.6 %collective-permute-start.8 = (f32[4,256,128]{2,1,0:T(8,128)S(1)}, f32[4,256,128]{2,1,0:T(8,128)S(1)}, u32[]{:S(2)}, u32[]{:S(2)}) collective-permute-start(f32[4,256,128]{2,1,0:T(8,128)S(1)} %get-tuple-element.43.refs_4_), channel_id=1, source_target_pairs={{0,32},{16,48},{32,0},{48,16},{64,96},{80,112},{96,64},{112,80},{1... | collective-permute-start | bytes 1572872 | tf_op jit(solution)/shard_map/ppermute | solution.py:42
  35.8 13.3 %collective-permute-start.10 = (f32[768,128]{1,0:T(8,128)S(1)}, f32[768,128]{1,0:T(8,128)S(1)}, u32[]{:S(2)}, u32[]{:S(2)}) collective-permute-start(f32[768,128]{1,0:T(8,128)S(1)} %get-tuple-element.45.refs_3_), channel_id=1, source_target_pairs={{0,192},{16,208},{32,224},{48,240},{64,128},{80,144},{96,160},{112... | collective-permute-start | bytes 1179656 | tf_op jit(solution)/shard_map/ppermute | solution.py:42
  38.0 12.1 %collective-permute-start.9 = (f32[768,128]{1,0:T(8,128)S(1)}, f32[768,128]{1,0:T(8,128)S(1)}, u32[]{:S(2)}, u32[]{:S(2)}) collective-permute-start(f32[768,128]{1,0:T(8,128)S(1)} %get-tuple-element.44.refs_2_), channel_id=1, source_target_pairs={{0,64},{16,80},{32,96},{48,112},{64,0},{80,16},{96,32},{112,48},{1... | collective-permute-start | bytes 1179656 | tf_op jit(solution)/shard_map/ppermute | solution.py:42
  38.3 15.0 %collective-permute-start.6 = (f32[2,256,128]{2,1,0:T(8,128)S(1)}, f32[2,256,128]{2,1,0:T(8,128)S(1)}, u32[]{:S(2)}, u32[]{:S(2)}) collective-permute-start(f32[2,256,128]{2,1,0:T(8,128)S(1)} %get-tuple-element.47), channel_id=1, source_target_pairs={{0,64},{16,80},{32,96},{48,112},{64,0},{80,16},{96,32},{112,48},{1... | collective-permute-start | bytes 786440 | tf_op jit(solution)/shard_map/ppermute | solution.py:42
  40.2 13.0 %collective-permute-start.7 = (f32[2,256,128]{2,1,0:T(8,128)S(1)}, f32[2,256,128]{2,1,0:T(8,128)S(1)}, u32[]{:S(2)}, u32[]{:S(2)}) collective-permute-start(f32[2,256,128]{2,1,0:T(8,128)S(1)} %get-tuple-element.48), channel_id=1, source_target_pairs={{0,192},{16,208},{32,224},{48,240},{64,128},{80,144},{96,160},{112... | collective-permute-start | bytes 786440 | tf_op jit(solution)/shard_map/ppermute | solution.py:42
  50.2 13.5 %collective-permute-start.14 = (f32[768,128]{1,0:T(8,128)S(1)}, f32[768,128]{1,0:T(8,128)S(1)}, u32[]{:S(2)}, u32[]{:S(2)}) collective-permute-start(f32[768,128]{1,0:T(8,128)S(1)} %get-tuple-element.52.refs_6_), channel_id=1, source_target_pairs={{0,32},{16,48},{32,0},{48,16},{64,96},{80,112},{96,64},{112,80},{1... | collective-permute-start | bytes 1179656 | tf_op jit(solution)/shard_map/ppermute | solution.py:42
  53.4 10.1 %collective-permute-start.11 = (f32[512,128]{1,0:T(8,128)S(1)}, f32[512,128]{1,0:T(8,128)S(1)}, u32[]{:S(2)}, u32[]{:S(2)}) collective-permute-start(f32[512,128]{1,0:T(8,128)S(1)} %get-tuple-element.54), channel_id=1, source_target_pairs={{0,64},{16,80},{32,96},{48,112},{64,0},{80,16},{96,32},{112,48},{1... | collective-permute-start | bytes 786440 | tf_op jit(solution)/shard_map/ppermute | solution.py:42
  53.7 9.9 %collective-permute-start.12 = (f32[512,128]{1,0:T(8,128)S(1)}, f32[512,128]{1,0:T(8,128)S(1)}, u32[]{:S(2)}, u32[]{:S(2)}) collective-permute-start(f32[512,128]{1,0:T(8,128)S(1)} %get-tuple-element.55), channel_id=1, source_target_pairs={{0,192},{16,208},{32,224},{48,240},{64,128},{80,144},{96,160},{112... | collective-permute-start | bytes 786440 | tf_op jit(solution)/shard_map/ppermute | solution.py:42
  55.0 8.5 %collective-permute-start.13 = (f32[256,128]{1,0:T(8,128)S(1)}, f32[256,128]{1,0:T(8,128)S(1)}, u32[]{:S(2)}, u32[]{:S(2)}) collective-permute-start(f32[256,128]{1,0:T(8,128)S(1)} %get-tuple-element.56), channel_id=1, source_target_pairs={{0,128},{16,144},{32,160},{48,176},{64,192},{80,208},{96,224},{112... | collective-permute-start | bytes 393224 | tf_op jit(solution)/shard_map/ppermute | solution.py:42

commit v4 on v3

--- a/solution.py
+++ b/solution.py
@@ -13,7 +13,7 @@
 X, Y, CORES = 4, 2, 2
 OWNERS = 16
 STEPS = OWNERS // 2
-WAITS = ((0, 1), (1, 3), (3, STEPS))
+WAITS = ((0, 2), (2, STEPS))
 LAYER = 6
 FIRST = 4
 ROOM = (50, 32, 32)
@@ -122,7 +122,7 @@
             for step in range(begin, end):
                 one_step(step, 0)
     else:
-        lax.fori_loop(0, STEPS, one_step, 0, unroll=4)
+        lax.fori_loop(0, STEPS, one_step, 0, unroll=True)
 
 
 def gradients(me, hidden, upstream, share, along_y_first, room, streamed, after=()):

time: 88.3 us -> 88.2 us (level)
  transfers between devices with their start and end apart: 15 -> 15, of which waited for: 11 -> 11; matrix products, arithmetic and copies ran while one was open for 0% -> 0% of each run, Pallas kernels for 6% -> 5%
where the time goes in v4:
time: 88.2 us; the launch traced here: 88 us
  waiting for transfers between devices  35.1 us (40%)
  blocking collectives  22.3 us (25%)
  starting transfers between devices  17.1 us (19%)
  Pallas kernels  11.9 us (13%)
    ppermute x15, waiting for transfers between devices, send(): return lax.ppermute(array, 'intra', pairs)  35.1 us
    all_to_all x1, blocking collectives, body(): lax.all_to_all(node, 'inter', split_axis=0, concat_axis=0, tiled=True)  22.3 us
    ppermute x15, starting transfers between devices, send(): return lax.ppermute(array, 'intra', pairs)  17.1 us
    pallas_call x3, Pallas kernels, gradients(): pl.pallas_call(functools.partial(gradient_kernel, share, along_y_first, l...  8.73 us
  transfers between devices with their start and end apart: 15, of which 11 were waited for; matrix products, arithmetic and copies ran while one was open for 0% of the time, Pallas kernels for 5%

profile of v4, /device:TPU:32, one launch (start us, length us, event | category | flops | bytes accessed | tf_op | source)
XLA Modules:
  0.0 88.0 jit_solution(16521846144252027391)
XLA Ops:
  0.6 0.0 copy-start.2
  0.6 0.7 copy-done.2
  1.4 0.0 copy-start
  1.4 4.8 %shard_map.60 = (bf16[8,768,128]{2,1,0:T(8,128)(2,1)S(1)}, bf16[8,768,128]{2,1,0:T(8,128)(2,1)S(1)}) custom-call(s32[1]{0:T(128)} %bitcast.me_ref, bf16[128,128]{1,0:T(8,128)(2,1)S(1)} %copy-done.2, bf16[128,12288]{1,0:T(8,128)(2,1)} %upstream_ref.4), custom_call_target="tpu_custom_call" | custom-call | flops 1 | bytes 1 | tf_op jit(solution)/shard_map/pallas_call | solution.py:135
  6.2 0.1 collective-permute-start.1
  6.3 0.0 copy-done
  6.3 0.0 copy-done.1
  6.3 2.6 %shard_map.59 = (bf16[8,512,128]{2,1,0:T(8,128)(2,1)S(1)}, bf16[8,512,128]{2,1,0:T(8,128)(2,1)S(1)}) custom-call(s32[1]{0:T(128)} %bitcast.me_ref, bf16[128,128]{1,0:T(8,128)(2,1)S(1)} %copy-done.1, bf16[128,12288]{1,0:T(8,128)(2,1)S(1)} %copy-done), custom_call_target="tpu_custom_call" | custom-call | flops 1 | bytes 1 | tf_op jit(solution)/shard_map/pallas_call | solution.py:135
  8.9 0.6 collective-permute-start
  9.4 0.3 collective-permute-done.1
  9.7 0.3 shard_map.61
  10.0 1.7 %collective-permute-done.refs_1_ = bf16[8,512,128]{2,1,0:T(8,128)(2,1)S(1)} collective-permute-done((bf16[8,512,128]{2,1,0:T(8,128)(2,1)S(1)}, bf16[8,512,128]{2,1,0:T(8,128)(2,1)S(1)}, u32[]{:S(2)}, u32[]{:S(2)}) %collective-permute-start) | collective-permute-done | bytes 1048608 | tf_op jit(solution)/shard_map/ppermute | solution.py:42
  11.7 0.2 shard_map.62
  11.9 1.7 %collective-permute-start.2 = (f32[4,512,128]{2,1,0:T(8,128)S(1)}, f32[4,512,128]{2,1,0:T(8,128)S(1)}, u32[]{:S(2)}, u32[]{:S(2)}) collective-permute-start(f32[4,512,128]{2,1,0:T(8,128)S(1)} %get-tuple-element.36), channel_id=1, source_target_pairs={{0,32},{16,48},{32,0},{48,16},{64,96},{80,112},{96,64},{112,80},{1... | collective-permute-start | bytes 3145736 | tf_op jit(solution)/shard_map/ppermute | solution.py:42
  13.6 1.5 %collective-permute-start.3 = (f32[2,768,128]{2,1,0:T(8,128)S(1)}, f32[2,768,128]{2,1,0:T(8,128)S(1)}, u32[]{:S(2)}, u32[]{:S(2)}) collective-permute-start(f32[2,768,128]{2,1,0:T(8,128)S(1)} %get-tuple-element.39), channel_id=1, source_target_pairs={{0,64},{16,80},{32,96},{48,112},{64,0},{80,16},{96,32},{112,48},{1... | collective-permute-start | bytes 2359304 | tf_op jit(solution)/shard_map/ppermute | solution.py:42
  15.1 2.1 %collective-permute-start.4 = (f32[2,768,128]{2,1,0:T(8,128)S(1)}, f32[2,768,128]{2,1,0:T(8,128)S(1)}, u32[]{:S(2)}, u32[]{:S(2)}) collective-permute-start(f32[2,768,128]{2,1,0:T(8,128)S(1)} %get-tuple-element.40), channel_id=1, source_target_pairs={{0,192},{16,208},{32,224},{48,240},{64,128},{80,144},{96,160},{112... | collective-permute-start | bytes 2359304 | tf_op jit(solution)/shard_map/ppermute | solution.py:42
  17.2 1.4 %shard_map.63 = (bf16[8,256,128]{2,1,0:T(8,128)(2,1)S(1)}, bf16[8,256,128]{2,1,0:T(8,128)(2,1)S(1)}) custom-call(s32[1]{0:T(128)} %bitcast.me_ref, bf16[128,128]{1,0:T(8,128)(2,1)S(1)} %copy-done.1, bf16[128,12288]{1,0:T(8,128)(2,1)S(1)} %copy-done, f32[4,512,128]{2,1,0:T(8,128)S(1)} %get-tuple-element.35.refs_0_), custom_call_target="tpu_custom_call" | custom-call | flops 1 | bytes 1 | tf_op jit(solution)/shard_map/pallas_call | solution.py:135
  18.6 0.1 collective-permute-start.5
  18.7 1.9 %collective-permute-done.5.refs_1_ = bf16[8,256,128]{2,1,0:T(8,128)(2,1)S(1)} collective-permute-done((bf16[8,256,128]{2,1,0:T(8,128)(2,1)S(1)}, bf16[8,256,128]{2,1,0:T(8,128)(2,1)S(1)}, u32[]{:S(2)}, u32[]{:S(2)}) %collective-permute-start.5) | collective-permute-done | bytes 524320 | tf_op jit(solution)/shard_map/ppermute | solution.py:42
  20.6 0.1 shard_map.64
  20.7 0.5 collective-permute-start.8
  21.3 11.9 %collective-permute-done.3.refs_2_.refs_1_ = f32[2,768,128]{2,1,0:T(8,128)S(1)} collective-permute-done((f32[2,768,128]{2,1,0:T(8,128)S(1)}, f32[2,768,128]{2,1,0:T(8,128)S(1)}, u32[]{:S(2)}, u32[]{:S(2)}) %collective-permute-start.3) | collective-permute-done | bytes 786464 | tf_op jit(solution)/shard_map/ppermute | solution.py:42
  33.1 2.4 %collective-permute-done.4.refs_3_.refs_2_ = f32[2,768,128]{2,1,0:T(8,128)S(1)} collective-permute-done((f32[2,768,128]{2,1,0:T(8,128)S(1)}, f32[2,768,128]{2,1,0:T(8,128)S(1)}, u32[]{:S(2)}, u32[]{:S(2)}) %collective-permute-start.4) | collective-permute-done | bytes 786464 | tf_op jit(solution)/shard_map/ppermute | solution.py:42
  35.6 0.1 shard_map.65
  35.7 2.2 %collective-permute-start.10 = (f32[768,128]{1,0:T(8,128)S(1)}, f32[768,128]{1,0:T(8,128)S(1)}, u32[]{:S(2)}, u32[]{:S(2)}) collective-permute-start(f32[768,128]{1,0:T(8,128)S(1)} %get-tuple-element.45.refs_3_), channel_id=1, source_target_pairs={{0,192},{16,208},{32,224},{48,240},{64,128},{80,144},{96,160},{112... | collective-permute-start | bytes 1179656 | tf_op jit(solution)/shard_map/ppermute | solution.py:42
  37.9 0.0 collective-permute-start.9
  37.9 0.2 collective-permute-done.2
  38.0 0.1 shard_map.66
  38.1 2.0 %collective-permute-start.6 = (f32[2,256,128]{2,1,0:T(8,128)S(1)}, f32[2,256,128]{2,1,0:T(8,128)S(1)}, u32[]{:S(2)}, u32[]{:S(2)}) collective-permute-start(f32[2,256,128]{2,1,0:T(8,128)S(1)} %get-tuple-element.47), channel_id=1, source_target_pairs={{0,64},{16,80},{32,96},{48,112},{64,0},{80,16},{96,32},{112,48},{1... | collective-permute-start | bytes 786440 | tf_op jit(solution)/shard_map/ppermute | solution.py:42
  40.1 1.7 %collective-permute-start.7 = (f32[2,256,128]{2,1,0:T(8,128)S(1)}, f32[2,256,128]{2,1,0:T(8,128)S(1)}, u32[]{:S(2)}, u32[]{:S(2)}) collective-permute-start(f32[2,256,128]{2,1,0:T(8,128)S(1)} %get-tuple-element.48), channel_id=1, source_target_pairs={{0,192},{16,208},{32,224},{48,240},{64,128},{80,144},{96,160},{112... | collective-permute-start | bytes 786440 | tf_op jit(solution)/shard_map/ppermute | solution.py:42
  41.8 7.2 %collective-permute-done.10.refs_4_ = f32[768,128]{1,0:T(8,128)S(1)} collective-permute-done((f32[768,128]{1,0:T(8,128)S(1)}, f32[768,128]{1,0:T(8,128)S(1)}, u32[]{:S(2)}, u32[]{:S(2)}) %collective-permute-start.10) | collective-permute-done | bytes 393248 | tf_op jit(solution)/shard_map/ppermute | solution.py:42
  49.0 0.9 %collective-permute-done.9.refs_3_ = f32[768,128]{1,0:T(8,128)S(1)} collective-permute-done((f32[768,128]{1,0:T(8,128)S(1)}, f32[768,128]{1,0:T(8,128)S(1)}, u32[]{:S(2)}, u32[]{:S(2)}) %collective-permute-start.9) | collective-permute-done | bytes 393248 | tf_op jit(solution)/shard_map/ppermute | solution.py:42
  49.9 0.1 shard_map.67
  50.0 0.5 collective-permute-start.14
  50.6 0.0 collective-permute-done.8.refs_1_
  50.6 2.6 %collective-permute-done.6.refs_4_.refs_1_ = f32[2,256,128]{2,1,0:T(8,128)S(1)} collective-permute-done((f32[2,256,128]{2,1,0:T(8,128)S(1)}, f32[2,256,128]{2,1,0:T(8,128)S(1)}, u32[]{:S(2)}, u32[]{:S(2)}) %collective-permute-start.6) | collective-permute-done | bytes 262176 | tf_op jit(solution)/shard_map/ppermute | solution.py:42
  53.1 0.0 collective-permute-done.7.refs_5_.refs_2_
  53.1 0.1 shard_map.68
  53.2 0.4 collective-permute-start.11
  53.6 1.3 %collective-permute-start.12 = (f32[512,128]{1,0:T(8,128)S(1)}, f32[512,128]{1,0:T(8,128)S(1)}, u32[]{:S(2)}, u32[]{:S(2)}) collective-permute-start(f32[512,128]{1,0:T(8,128)S(1)} %get-tuple-element.55), channel_id=1, source_target_pairs={{0,192},{16,208},{32,224},{48,240},{64,128},{80,144},{96,160},{112... | collective-permute-start | bytes 786440 | tf_op jit(solution)/shard_map/ppermute | solution.py:42
  54.9 2.5 %collective-permute-start.13 = (f32[256,128]{1,0:T(8,128)S(1)}, f32[256,128]{1,0:T(8,128)S(1)}, u32[]{:S(2)}, u32[]{:S(2)}) collective-permute-start(f32[256,128]{1,0:T(8,128)S(1)} %get-tuple-element.56), channel_id=1, source_target_pairs={{0,128},{16,144},{32,160},{48,176},{64,192},{80,208},{96,224},{112... | collective-permute-start | bytes 393224 | tf_op jit(solution)/shard_map/ppermute | solution.py:42
  57.4 6.0 %collective-permute-done.13.refs_6_ = f32[256,128]{1,0:T(8,128)S(1)} collective-permute-done((f32[256,128]{1,0:T(8,128)S(1)}, f32[256,128]{1,0:T(8,128)S(1)}, u32[]{:S(2)}, u32[]{:S(2)}) %collective-permute-start.13) | collective-permute-done | bytes 131104 | tf_op jit(solution)/shard_map/ppermute | solution.py:42
  63.4 0.0 collective-permute-done.11.refs_4_
  63.4 0.2 collective-permute-done.12.refs_5_
  63.5 0.0 collective-permute-done.14.refs_8_
  63.5 0.4 shard_map.69
  64.0 22.3 %all_to_all.5.pieces_ref = bf16[16,96,128]{2,1,0:T(8,128)(2,1)} all-to-all(bf16[16,96,128]{2,1,0:T(8,128)(2,1)S(1)} %shard_map.69), channel_id=1, replica_groups=mesh['intra'=16,'inter'=16] {'inter'}, dimensions={0} | all-to-all | bytes 786432 | tf_op jit(solution)/shard_map/all_to_all | solution.py:319
  86.3 1.7 %shard_map.70 = (f32[8,768]{1,0:T(8,128)}, f32[8,768]{1,0:T(8,128)}) custom-call(bf16[16,96,128]{2,1,0:T(8,128)(2,1)} %all_to_all.5.pieces_ref), custom_call_target="tpu_custom_call" | custom-call | tf_op jit(solution)/shard_map/pallas_call | solution.py:322
  (1 shorter events, 0.0 us)
Async XLA Ops:
  0.6 0.8 copy-start.2
  1.4 4.9 %copy-start = (bf16[128,12288]{1,0:T(8,128)(2,1)S(1)}, bf16[128,12288]{1,0:T(8,128)(2,1)}, u32[]{:S(2)}) copy-start(bf16[128,12288]{1,0:T(8,128)(2,1)} %upstream_ref.5) | copy-start | bytes 9437188
  1.4 4.9 %copy-start.1 = (bf16[128,128]{1,0:T(8,128)(2,1)S(1)}, bf16[128,128]{1,0:T(8,128)(2,1)}, u32[]{:S(2)}) copy-start(bf16[128,128]{1,0:T(8,128)(2,1)} %hidden_ref.5) | copy-start | bytes 98308
  6.2 3.5 %collective-permute-start.1 = (bf16[8,768,128]{2,1,0:T(8,128)(2,1)S(1)}, bf16[8,768,128]{2,1,0:T(8,128)(2,1)S(1)}, u32[]{:S(2)}, u32[]{:S(2)}) collective-permute-start(bf16[8,768,128]{2,1,0:T(8,128)(2,1)S(1)} %get-tuple-element.33), channel_id=1, source_target_pairs={{0,16},{16,0},{32,48},{48,32},{64,80},{80,64},{96,112},{112,96},{1... | collective-permute-start | bytes 4718600 | tf_op jit(solution)/shard_map/ppermute | solution.py:42
  8.9 2.9 %collective-permute-start = (bf16[8,512,128]{2,1,0:T(8,128)(2,1)S(1)}, bf16[8,512,128]{2,1,0:T(8,128)(2,1)S(1)}, u32[]{:S(2)}, u32[]{:S(2)}) collective-permute-start(bf16[8,512,128]{2,1,0:T(8,128)(2,1)S(1)} %get-tuple-element.31), channel_id=1, source_target_pairs={{0,16},{16,0},{32,48},{48,32},{64,80},{80,64},{96,112},{112,96},{1... | collective-permute-start | bytes 3145736 | tf_op jit(solution)/shard_map/ppermute | solution.py:42
  11.9 26.1 %collective-permute-start.2 = (f32[4,512,128]{2,1,0:T(8,128)S(1)}, f32[4,512,128]{2,1,0:T(8,128)S(1)}, u32[]{:S(2)}, u32[]{:S(2)}) collective-permute-start(f32[4,512,128]{2,1,0:T(8,128)S(1)} %get-tuple-element.36), channel_id=1, source_target_pairs={{0,32},{16,48},{32,0},{48,16},{64,96},{80,112},{96,64},{112,80},{1... | collective-permute-start | bytes 3145736 | tf_op jit(solution)/shard_map/ppermute | solution.py:42
  13.6 19.5 %collective-permute-start.3 = (f32[2,768,128]{2,1,0:T(8,128)S(1)}, f32[2,768,128]{2,1,0:T(8,128)S(1)}, u32[]{:S(2)}, u32[]{:S(2)}) collective-permute-start(f32[2,768,128]{2,1,0:T(8,128)S(1)} %get-tuple-element.39), channel_id=1, source_target_pairs={{0,64},{16,80},{32,96},{48,112},{64,0},{80,16},{96,32},{112,48},{1... | collective-permute-start | bytes 2359304 | tf_op jit(solution)/shard_map/ppermute | solution.py:42
  15.1 20.5 %collective-permute-start.4 = (f32[2,768,128]{2,1,0:T(8,128)S(1)}, f32[2,768,128]{2,1,0:T(8,128)S(1)}, u32[]{:S(2)}, u32[]{:S(2)}) collective-permute-start(f32[2,768,128]{2,1,0:T(8,128)S(1)} %get-tuple-element.40), channel_id=1, source_target_pairs={{0,192},{16,208},{32,224},{48,240},{64,128},{80,144},{96,160},{112... | collective-permute-start | bytes 2359304 | tf_op jit(solution)/shard_map/ppermute | solution.py:42
  18.6 2.0 %collective-permute-start.5 = (bf16[8,256,128]{2,1,0:T(8,128)(2,1)S(1)}, bf16[8,256,128]{2,1,0:T(8,128)(2,1)S(1)}, u32[]{:S(2)}, u32[]{:S(2)}) collective-permute-start(bf16[8,256,128]{2,1,0:T(8,128)(2,1)S(1)} %get-tuple-element.42), channel_id=1, source_target_pairs={{0,16},{16,0},{32,48},{48,32},{64,80},{80,64},{96,112},{112,96},{1... | collective-permute-start | bytes 1572872 | tf_op jit(solution)/shard_map/ppermute | solution.py:42
  20.7 29.8 %collective-permute-start.8 = (f32[4,256,128]{2,1,0:T(8,128)S(1)}, f32[4,256,128]{2,1,0:T(8,128)S(1)}, u32[]{:S(2)}, u32[]{:S(2)}) collective-permute-start(f32[4,256,128]{2,1,0:T(8,128)S(1)} %get-tuple-element.43.refs_4_), channel_id=1, source_target_pairs={{0,32},{16,48},{32,0},{48,16},{64,96},{80,112},{96,64},{112,80},{1... | collective-permute-start | bytes 1572872 | tf_op jit(solution)/shard_map/ppermute | solution.py:42
  35.7 13.3 %collective-permute-start.10 = (f32[768,128]{1,0:T(8,128)S(1)}, f32[768,128]{1,0:T(8,128)S(1)}, u32[]{:S(2)}, u32[]{:S(2)}) collective-permute-start(f32[768,128]{1,0:T(8,128)S(1)} %get-tuple-element.45.refs_3_), channel_id=1, source_target_pairs={{0,192},{16,208},{32,224},{48,240},{64,128},{80,144},{96,160},{112... | collective-permute-start | bytes 1179656 | tf_op jit(solution)/shard_map/ppermute | solution.py:42
  37.9 12.1 %collective-permute-start.9 = (f32[768,128]{1,0:T(8,128)S(1)}, f32[768,128]{1,0:T(8,128)S(1)}, u32[]{:S(2)}, u32[]{:S(2)}) collective-permute-start(f32[768,128]{1,0:T(8,128)S(1)} %get-tuple-element.44.refs_2_), channel_id=1, source_target_pairs={{0,64},{16,80},{32,96},{48,112},{64,0},{80,16},{96,32},{112,48},{1... | collective-permute-start | bytes 1179656 | tf_op jit(solution)/shard_map/ppermute | solution.py:42
  38.1 15.0 %collective-permute-start.6 = (f32[2,256,128]{2,1,0:T(8,128)S(1)}, f32[2,256,128]{2,1,0:T(8,128)S(1)}, u32[]{:S(2)}, u32[]{:S(2)}) collective-permute-start(f32[2,256,128]{2,1,0:T(8,128)S(1)} %get-tuple-element.47), channel_id=1, source_target_pairs={{0,64},{16,80},{32,96},{48,112},{64,0},{80,16},{96,32},{112,48},{1... | collective-permute-start | bytes 786440 | tf_op jit(solution)/shard_map/ppermute | solution.py:42
  40.1 13.0 %collective-permute-start.7 = (f32[2,256,128]{2,1,0:T(8,128)S(1)}, f32[2,256,128]{2,1,0:T(8,128)S(1)}, u32[]{:S(2)}, u32[]{:S(2)}) collective-permute-start(f32[2,256,128]{2,1,0:T(8,128)S(1)} %get-tuple-element.48), channel_id=1, source_target_pairs={{0,192},{16,208},{32,224},{48,240},{64,128},{80,144},{96,160},{112... | collective-permute-start | bytes 786440 | tf_op jit(solution)/shard_map/ppermute | solution.py:42
  50.0 13.5 %collective-permute-start.14 = (f32[768,128]{1,0:T(8,128)S(1)}, f32[768,128]{1,0:T(8,128)S(1)}, u32[]{:S(2)}, u32[]{:S(2)}) collective-permute-start(f32[768,128]{1,0:T(8,128)S(1)} %get-tuple-element.52.refs_6_), channel_id=1, source_target_pairs={{0,32},{16,48},{32,0},{48,16},{64,96},{80,112},{96,64},{112,80},{1... | collective-permute-start | bytes 1179656 | tf_op jit(solution)/shard_map/ppermute | solution.py:42
  53.2 10.1 %collective-permute-start.11 = (f32[512,128]{1,0:T(8,128)S(1)}, f32[512,128]{1,0:T(8,128)S(1)}, u32[]{:S(2)}, u32[]{:S(2)}) collective-permute-start(f32[512,128]{1,0:T(8,128)S(1)} %get-tuple-element.54), channel_id=1, source_target_pairs={{0,64},{16,80},{32,96},{48,112},{64,0},{80,16},{96,32},{112,48},{1... | collective-permute-start | bytes 786440 | tf_op jit(solution)/shard_map/ppermute | solution.py:42
  53.6 9.9 %collective-permute-start.12 = (f32[512,128]{1,0:T(8,128)S(1)}, f32[512,128]{1,0:T(8,128)S(1)}, u32[]{:S(2)}, u32[]{:S(2)}) collective-permute-start(f32[512,128]{1,0:T(8,128)S(1)} %get-tuple-element.55), channel_id=1, source_target_pairs={{0,192},{16,208},{32,224},{48,240},{64,128},{80,144},{96,160},{112... | collective-permute-start | bytes 786440 | tf_op jit(solution)/shard_map/ppermute | solution.py:42
  54.9 8.5 %collective-permute-start.13 = (f32[256,128]{1,0:T(8,128)S(1)}, f32[256,128]{1,0:T(8,128)S(1)}, u32[]{:S(2)}, u32[]{:S(2)}) collective-permute-start(f32[256,128]{1,0:T(8,128)S(1)} %get-tuple-element.56), channel_id=1, source_target_pairs={{0,128},{16,144},{32,160},{48,176},{64,192},{80,208},{96,224},{112... | collective-permute-start | bytes 393224 | tf_op jit(solution)/shard_map/ppermute | solution.py:42

commit v5 on v4

--- a/solution.py
+++ b/solution.py
@@ -163,7 +163,7 @@
             kernel(*[view(ref, step) for ref in used])
             return carry
 
-        lax.fori_loop(0, steps, one_step, 0)
+        lax.fori_loop(0, steps, one_step, 0, unroll=True)
 
     return pl.pallas_call(
         whole if steps > 1 else lambda *refs: kernel(*refs[: len(ins)], *refs[len(ins) + len(after) :]),

time: 88.2 us -> 88.4 us (level)
  transfers between devices with their start and end apart: 15 -> 15, of which waited for: 11 -> 10; matrix products, arithmetic and copies ran while one was open for 0% -> 0% of each run, Pallas kernels for 5% -> 5%
where the time goes in v5:
time: 88.4 us; the launch traced here: 88.1 us
  waiting for transfers between devices  35.2 us (40%)
  blocking collectives  22.3 us (25%)
  starting transfers between devices  17.3 us (20%)
  Pallas kernels  11.8 us (13%)
    ppermute x15, waiting for transfers between devices, send(): return lax.ppermute(array, 'intra', pairs)  35.2 us
    all_to_all x1, blocking collectives, body(): lax.all_to_all(node, 'inter', split_axis=0, concat_axis=0, tiled=True)  22.3 us
    ppermute x15, starting transfers between devices, send(): return lax.ppermute(array, 'intra', pairs)  17.3 us
    pallas_call x3, Pallas kernels, gradients(): pl.pallas_call(functools.partial(gradient_kernel, share, along_y_first, l...  8.73 us
  transfers between devices with their start and end apart: 15, of which 10 were waited for; matrix products, arithmetic and copies ran while one was open for 0% of the time, Pallas kernels for 5%

profile of v5, /device:TPU:32, one launch (start us, length us, event | category | flops | bytes accessed | tf_op | source)
XLA Modules:
  0.0 88.1 jit_solution(3664127244171862557)
XLA Ops:
  0.6 0.0 copy-start.2
  0.6 0.7 copy-done.2
  1.4 0.0 copy-start
  1.4 4.8 %shard_map.60 = (bf16[8,768,128]{2,1,0:T(8,128)(2,1)S(1)}, bf16[8,768,128]{2,1,0:T(8,128)(2,1)S(1)}) custom-call(s32[1]{0:T(128)} %bitcast.me_ref, bf16[128,128]{1,0:T(8,128)(2,1)S(1)} %copy-done.2, bf16[128,12288]{1,0:T(8,128)(2,1)} %upstream_ref.4), custom_call_target="tpu_custom_call" | custom-call | flops 1 | bytes 1 | tf_op jit(solution)/shard_map/pallas_call | solution.py:135
  6.2 0.1 collective-permute-start.1
  6.3 0.0 copy-done
  6.3 0.0 copy-done.1
  6.3 2.6 %shard_map.59 = (bf16[8,512,128]{2,1,0:T(8,128)(2,1)S(1)}, bf16[8,512,128]{2,1,0:T(8,128)(2,1)S(1)}) custom-call(s32[1]{0:T(128)} %bitcast.me_ref, bf16[128,128]{1,0:T(8,128)(2,1)S(1)} %copy-done.1, bf16[128,12288]{1,0:T(8,128)(2,1)S(1)} %copy-done), custom_call_target="tpu_custom_call" | custom-call | flops 1 | bytes 1 | tf_op jit(solution)/shard_map/pallas_call | solution.py:135
  8.9 0.6 collective-permute-start
  9.4 0.3 collective-permute-done.1
  9.7 0.3 shard_map.61
  10.0 1.7 %collective-permute-done.refs_1_ = bf16[8,512,128]{2,1,0:T(8,128)(2,1)S(1)} collective-permute-done((bf16[8,512,128]{2,1,0:T(8,128)(2,1)S(1)}, bf16[8,512,128]{2,1,0:T(8,128)(2,1)S(1)}, u32[]{:S(2)}, u32[]{:S(2)}) %collective-permute-start) | collective-permute-done | bytes 1048608 | tf_op jit(solution)/shard_map/ppermute | solution.py:42
  11.7 0.2 shard_map.62
  11.9 1.7 %collective-permute-start.2 = (f32[4,512,128]{2,1,0:T(8,128)S(1)}, f32[4,512,128]{2,1,0:T(8,128)S(1)}, u32[]{:S(2)}, u32[]{:S(2)}) collective-permute-start(f32[4,512,128]{2,1,0:T(8,128)S(1)} %get-tuple-element.36), channel_id=1, source_target_pairs={{0,32},{16,48},{32,0},{48,16},{64,96},{80,112},{96,64},{112,80},{1... | collective-permute-start | bytes 3145736 | tf_op jit(solution)/shard_map/ppermute | solution.py:42
  13.6 1.5 %collective-permute-start.3 = (f32[2,768,128]{2,1,0:T(8,128)S(1)}, f32[2,768,128]{2,1,0:T(8,128)S(1)}, u32[]{:S(2)}, u32[]{:S(2)}) collective-permute-start(f32[2,768,128]{2,1,0:T(8,128)S(1)} %get-tuple-element.39), channel_id=1, source_target_pairs={{0,64},{16,80},{32,96},{48,112},{64,0},{80,16},{96,32},{112,48},{1... | collective-permute-start | bytes 2359304 | tf_op jit(solution)/shard_map/ppermute | solution.py:42
  15.1 2.1 %collective-permute-start.4 = (f32[2,768,128]{2,1,0:T(8,128)S(1)}, f32[2,768,128]{2,1,0:T(8,128)S(1)}, u32[]{:S(2)}, u32[]{:S(2)}) collective-permute-start(f32[2,768,128]{2,1,0:T(8,128)S(1)} %get-tuple-element.40), channel_id=1, source_target_pairs={{0,192},{16,208},{32,224},{48,240},{64,128},{80,144},{96,160},{112... | collective-permute-start | bytes 2359304 | tf_op jit(solution)/shard_map/ppermute | solution.py:42
  17.2 1.4 %shard_map.63 = (bf16[8,256,128]{2,1,0:T(8,128)(2,1)S(1)}, bf16[8,256,128]{2,1,0:T(8,128)(2,1)S(1)}) custom-call(s32[1]{0:T(128)} %bitcast.me_ref, bf16[128,128]{1,0:T(8,128)(2,1)S(1)} %copy-done.1, bf16[128,12288]{1,0:T(8,128)(2,1)S(1)} %copy-done, f32[4,512,128]{2,1,0:T(8,128)S(1)} %get-tuple-element.35.refs_0_), custom_call_target="tpu_custom_call" | custom-call | flops 1 | bytes 1 | tf_op jit(solution)/shard_map/pallas_call | solution.py:135
  18.6 0.1 collective-permute-start.5
  18.7 1.9 %collective-permute-done.5.refs_1_ = bf16[8,256,128]{2,1,0:T(8,128)(2,1)S(1)} collective-permute-done((bf16[8,256,128]{2,1,0:T(8,128)(2,1)S(1)}, bf16[8,256,128]{2,1,0:T(8,128)(2,1)S(1)}, u32[]{:S(2)}, u32[]{:S(2)}) %collective-permute-start.5) | collective-permute-done | bytes 524320 | tf_op jit(solution)/shard_map/ppermute | solution.py:42
  20.6 0.1 shard_map.64
  20.7 0.5 collective-permute-start.8
  21.2 11.9 %collective-permute-done.3.refs_2_.refs_1_ = f32[2,768,128]{2,1,0:T(8,128)S(1)} collective-permute-done((f32[2,768,128]{2,1,0:T(8,128)S(1)}, f32[2,768,128]{2,1,0:T(8,128)S(1)}, u32[]{:S(2)}, u32[]{:S(2)}) %collective-permute-start.3) | collective-permute-done | bytes 786464 | tf_op jit(solution)/shard_map/ppermute | solution.py:42
  33.1 2.4 %collective-permute-done.4.refs_3_.refs_2_ = f32[2,768,128]{2,1,0:T(8,128)S(1)} collective-permute-done((f32[2,768,128]{2,1,0:T(8,128)S(1)}, f32[2,768,128]{2,1,0:T(8,128)S(1)}, u32[]{:S(2)}, u32[]{:S(2)}) %collective-permute-start.4) | collective-permute-done | bytes 786464 | tf_op jit(solution)/shard_map/ppermute | solution.py:42
  35.6 0.1 shard_map.65
  35.7 2.4 %collective-permute-start.10 = (f32[768,128]{1,0:T(8,128)S(1)}, f32[768,128]{1,0:T(8,128)S(1)}, u32[]{:S(2)}, u32[]{:S(2)}) collective-permute-start(f32[768,128]{1,0:T(8,128)S(1)} %get-tuple-element.45.refs_3_), channel_id=1, source_target_pairs={{0,192},{16,208},{32,224},{48,240},{64,128},{80,144},{96,160},{112... | collective-permute-start | bytes 1179656 | tf_op jit(solution)/shard_map/ppermute | solution.py:42
  38.0 0.0 collective-permute-start.9
  38.0 0.0 collective-permute-done.2
  38.0 0.1 shard_map.66
  38.1 2.1 %collective-permute-start.6 = (f32[2,256,128]{2,1,0:T(8,128)S(1)}, f32[2,256,128]{2,1,0:T(8,128)S(1)}, u32[]{:S(2)}, u32[]{:S(2)}) collective-permute-start(f32[2,256,128]{2,1,0:T(8,128)S(1)} %get-tuple-element.47), channel_id=1, source_target_pairs={{0,64},{16,80},{32,96},{48,112},{64,0},{80,16},{96,32},{112,48},{1... | collective-permute-start | bytes 786440 | tf_op jit(solution)/shard_map/ppermute | solution.py:42
  40.2 1.5 %collective-permute-start.7 = (f32[2,256,128]{2,1,0:T(8,128)S(1)}, f32[2,256,128]{2,1,0:T(8,128)S(1)}, u32[]{:S(2)}, u32[]{:S(2)}) collective-permute-start(f32[2,256,128]{2,1,0:T(8,128)S(1)} %get-tuple-element.48), channel_id=1, source_target_pairs={{0,192},{16,208},{32,224},{48,240},{64,128},{80,144},{96,160},{112... | collective-permute-start | bytes 786440 | tf_op jit(solution)/shard_map/ppermute | solution.py:42
  41.8 7.4 %collective-permute-done.10.refs_4_ = f32[768,128]{1,0:T(8,128)S(1)} collective-permute-done((f32[768,128]{1,0:T(8,128)S(1)}, f32[768,128]{1,0:T(8,128)S(1)}, u32[]{:S(2)}, u32[]{:S(2)}) %collective-permute-start.10) | collective-permute-done | bytes 393248 | tf_op jit(solution)/shard_map/ppermute | solution.py:42
  49.2 0.9 %collective-permute-done.9.refs_3_ = f32[768,128]{1,0:T(8,128)S(1)} collective-permute-done((f32[768,128]{1,0:T(8,128)S(1)}, f32[768,128]{1,0:T(8,128)S(1)}, u32[]{:S(2)}, u32[]{:S(2)}) %collective-permute-start.9) | collective-permute-done | bytes 393248 | tf_op jit(solution)/shard_map/ppermute | solution.py:42
  50.1 0.1 shard_map.67
  50.2 0.5 collective-permute-start.14
  50.7 0.0 collective-permute-done.8.refs_1_
  50.7 2.6 %collective-permute-done.6.refs_4_.refs_1_ = f32[2,256,128]{2,1,0:T(8,128)S(1)} collective-permute-done((f32[2,256,128]{2,1,0:T(8,128)S(1)}, f32[2,256,128]{2,1,0:T(8,128)S(1)}, u32[]{:S(2)}, u32[]{:S(2)}) %collective-permute-start.6) | collective-permute-done | bytes 262176 | tf_op jit(solution)/shard_map/ppermute | solution.py:42
  53.3 0.0 collective-permute-done.7.refs_5_.refs_2_
  53.3 0.1 shard_map.68
  53.4 0.4 collective-permute-start.11
  53.8 1.3 %collective-permute-start.12 = (f32[512,128]{1,0:T(8,128)S(1)}, f32[512,128]{1,0:T(8,128)S(1)}, u32[]{:S(2)}, u32[]{:S(2)}) collective-permute-start(f32[512,128]{1,0:T(8,128)S(1)} %get-tuple-element.55), channel_id=1, source_target_pairs={{0,192},{16,208},{32,224},{48,240},{64,128},{80,144},{96,160},{112... | collective-permute-start | bytes 786440 | tf_op jit(solution)/shard_map/ppermute | solution.py:42
  55.1 2.5 %collective-permute-start.13 = (f32[256,128]{1,0:T(8,128)S(1)}, f32[256,128]{1,0:T(8,128)S(1)}, u32[]{:S(2)}, u32[]{:S(2)}) collective-permute-start(f32[256,128]{1,0:T(8,128)S(1)} %get-tuple-element.56), channel_id=1, source_target_pairs={{0,128},{16,144},{32,160},{48,176},{64,192},{80,208},{96,224},{112... | collective-permute-start | bytes 393224 | tf_op jit(solution)/shard_map/ppermute | solution.py:42
  57.6 6.0 %collective-permute-done.13.refs_6_ = f32[256,128]{1,0:T(8,128)S(1)} collective-permute-done((f32[256,128]{1,0:T(8,128)S(1)}, f32[256,128]{1,0:T(8,128)S(1)}, u32[]{:S(2)}, u32[]{:S(2)}) %collective-permute-start.13) | collective-permute-done | bytes 131104 | tf_op jit(solution)/shard_map/ppermute | solution.py:42
  63.5 0.0 collective-permute-done.11.refs_4_
  63.5 0.2 collective-permute-done.12.refs_5_
  63.7 0.0 collective-permute-done.14.refs_8_
  63.7 0.4 shard_map.69
  64.1 22.3 %all_to_all.5.pieces_ref = bf16[16,96,128]{2,1,0:T(8,128)(2,1)} all-to-all(bf16[16,96,128]{2,1,0:T(8,128)(2,1)S(1)} %shard_map.69), channel_id=1, replica_groups=mesh['intra'=16,'inter'=16] {'inter'}, dimensions={0} | all-to-all | bytes 786432 | tf_op jit(solution)/shard_map/all_to_all | solution.py:319
  86.5 1.7 %shard_map.70 = (f32[8,768]{1,0:T(8,128)}, f32[8,768]{1,0:T(8,128)}) custom-call(bf16[16,96,128]{2,1,0:T(8,128)(2,1)} %all_to_all.5.pieces_ref), custom_call_target="tpu_custom_call" | custom-call | tf_op jit(solution)/shard_map/pallas_call | solution.py:322
  (1 shorter events, 0.0 us)
Async XLA Ops:
  0.6 0.8 copy-start.2
  1.4 4.9 %copy-start = (bf16[128,12288]{1,0:T(8,128)(2,1)S(1)}, bf16[128,12288]{1,0:T(8,128)(2,1)}, u32[]{:S(2)}) copy-start(bf16[128,12288]{1,0:T(8,128)(2,1)} %upstream_ref.5) | copy-start | bytes 9437188
  1.4 4.9 %copy-start.1 = (bf16[128,128]{1,0:T(8,128)(2,1)S(1)}, bf16[128,128]{1,0:T(8,128)(2,1)}, u32[]{:S(2)}) copy-start(bf16[128,128]{1,0:T(8,128)(2,1)} %hidden_ref.5) | copy-start | bytes 98308
  6.2 3.5 %collective-permute-start.1 = (bf16[8,768,128]{2,1,0:T(8,128)(2,1)S(1)}, bf16[8,768,128]{2,1,0:T(8,128)(2,1)S(1)}, u32[]{:S(2)}, u32[]{:S(2)}) collective-permute-start(bf16[8,768,128]{2,1,0:T(8,128)(2,1)S(1)} %get-tuple-element.33), channel_id=1, source_target_pairs={{0,16},{16,0},{32,48},{48,32},{64,80},{80,64},{96,112},{112,96},{1... | collective-permute-start | bytes 4718600 | tf_op jit(solution)/shard_map/ppermute | solution.py:42
  8.9 2.9 %collective-permute-start = (bf16[8,512,128]{2,1,0:T(8,128)(2,1)S(1)}, bf16[8,512,128]{2,1,0:T(8,128)(2,1)S(1)}, u32[]{:S(2)}, u32[]{:S(2)}) collective-permute-start(bf16[8,512,128]{2,1,0:T(8,128)(2,1)S(1)} %get-tuple-element.31), channel_id=1, source_target_pairs={{0,16},{16,0},{32,48},{48,32},{64,80},{80,64},{96,112},{112,96},{1... | collective-permute-start | bytes 3145736 | tf_op jit(solution)/shard_map/ppermute | solution.py:42
  11.9 26.1 %collective-permute-start.2 = (f32[4,512,128]{2,1,0:T(8,128)S(1)}, f32[4,512,128]{2,1,0:T(8,128)S(1)}, u32[]{:S(2)}, u32[]{:S(2)}) collective-permute-start(f32[4,512,128]{2,1,0:T(8,128)S(1)} %get-tuple-element.36), channel_id=1, source_target_pairs={{0,32},{16,48},{32,0},{48,16},{64,96},{80,112},{96,64},{112,80},{1... | collective-permute-start | bytes 3145736 | tf_op jit(solution)/shard_map/ppermute | solution.py:42
  13.6 19.5 %collective-permute-start.3 = (f32[2,768,128]{2,1,0:T(8,128)S(1)}, f32[2,768,128]{2,1,0:T(8,128)S(1)}, u32[]{:S(2)}, u32[]{:S(2)}) collective-permute-start(f32[2,768,128]{2,1,0:T(8,128)S(1)} %get-tuple-element.39), channel_id=1, source_target_pairs={{0,64},{16,80},{32,96},{48,112},{64,0},{80,16},{96,32},{112,48},{1... | collective-permute-start | bytes 2359304 | tf_op jit(solution)/shard_map/ppermute | solution.py:42
  15.1 20.5 %collective-permute-start.4 = (f32[2,768,128]{2,1,0:T(8,128)S(1)}, f32[2,768,128]{2,1,0:T(8,128)S(1)}, u32[]{:S(2)}, u32[]{:S(2)}) collective-permute-start(f32[2,768,128]{2,1,0:T(8,128)S(1)} %get-tuple-element.40), channel_id=1, source_target_pairs={{0,192},{16,208},{32,224},{48,240},{64,128},{80,144},{96,160},{112... | collective-permute-start | bytes 2359304 | tf_op jit(solution)/shard_map/ppermute | solution.py:42
  18.6 2.0 %collective-permute-start.5 = (bf16[8,256,128]{2,1,0:T(8,128)(2,1)S(1)}, bf16[8,256,128]{2,1,0:T(8,128)(2,1)S(1)}, u32[]{:S(2)}, u32[]{:S(2)}) collective-permute-start(bf16[8,256,128]{2,1,0:T(8,128)(2,1)S(1)} %get-tuple-element.42), channel_id=1, source_target_pairs={{0,16},{16,0},{32,48},{48,32},{64,80},{80,64},{96,112},{112,96},{1... | collective-permute-start | bytes 1572872 | tf_op jit(solution)/shard_map/ppermute | solution.py:42
  20.7 30.0 %collective-permute-start.8 = (f32[4,256,128]{2,1,0:T(8,128)S(1)}, f32[4,256,128]{2,1,0:T(8,128)S(1)}, u32[]{:S(2)}, u32[]{:S(2)}) collective-permute-start(f32[4,256,128]{2,1,0:T(8,128)S(1)} %get-tuple-element.43.refs_4_), channel_id=1, source_target_pairs={{0,32},{16,48},{32,0},{48,16},{64,96},{80,112},{96,64},{112,80},{1... | collective-permute-start | bytes 1572872 | tf_op jit(solution)/shard_map/ppermute | solution.py:42
  35.7 13.5 %collective-permute-start.10 = (f32[768,128]{1,0:T(8,128)S(1)}, f32[768,128]{1,0:T(8,128)S(1)}, u32[]{:S(2)}, u32[]{:S(2)}) collective-permute-start(f32[768,128]{1,0:T(8,128)S(1)} %get-tuple-element.45.refs_3_), channel_id=1, source_target_pairs={{0,192},{16,208},{32,224},{48,240},{64,128},{80,144},{96,160},{112... | collective-permute-start | bytes 1179656 | tf_op jit(solution)/shard_map/ppermute | solution.py:42
  38.0 12.1 %collective-permute-start.9 = (f32[768,128]{1,0:T(8,128)S(1)}, f32[768,128]{1,0:T(8,128)S(1)}, u32[]{:S(2)}, u32[]{:S(2)}) collective-permute-start(f32[768,128]{1,0:T(8,128)S(1)} %get-tuple-element.44.refs_2_), channel_id=1, source_target_pairs={{0,64},{16,80},{32,96},{48,112},{64,0},{80,16},{96,32},{112,48},{1... | collective-permute-start | bytes 1179656 | tf_op jit(solution)/shard_map/ppermute | solution.py:42
  38.1 15.2 %collective-permute-start.6 = (f32[2,256,128]{2,1,0:T(8,128)S(1)}, f32[2,256,128]{2,1,0:T(8,128)S(1)}, u32[]{:S(2)}, u32[]{:S(2)}) collective-permute-start(f32[2,256,128]{2,1,0:T(8,128)S(1)} %get-tuple-element.47), channel_id=1, source_target_pairs={{0,64},{16,80},{32,96},{48,112},{64,0},{80,16},{96,32},{112,48},{1... | collective-permute-start | bytes 786440 | tf_op jit(solution)/shard_map/ppermute | solution.py:42
  40.2 13.1 %collective-permute-start.7 = (f32[2,256,128]{2,1,0:T(8,128)S(1)}, f32[2,256,128]{2,1,0:T(8,128)S(1)}, u32[]{:S(2)}, u32[]{:S(2)}) collective-permute-start(f32[2,256,128]{2,1,0:T(8,128)S(1)} %get-tuple-element.48), channel_id=1, source_target_pairs={{0,192},{16,208},{32,224},{48,240},{64,128},{80,144},{96,160},{112... | collective-permute-start | bytes 786440 | tf_op jit(solution)/shard_map/ppermute | solution.py:42
  50.2 13.5 %collective-permute-start.14 = (f32[768,128]{1,0:T(8,128)S(1)}, f32[768,128]{1,0:T(8,128)S(1)}, u32[]{:S(2)}, u32[]{:S(2)}) collective-permute-start(f32[768,128]{1,0:T(8,128)S(1)} %get-tuple-element.52.refs_6_), channel_id=1, source_target_pairs={{0,32},{16,48},{32,0},{48,16},{64,96},{80,112},{96,64},{112,80},{1... | collective-permute-start | bytes 1179656 | tf_op jit(solution)/shard_map/ppermute | solution.py:42
  53.4 10.1 %collective-permute-start.11 = (f32[512,128]{1,0:T(8,128)S(1)}, f32[512,128]{1,0:T(8,128)S(1)}, u32[]{:S(2)}, u32[]{:S(2)}) collective-permute-start(f32[512,128]{1,0:T(8,128)S(1)} %get-tuple-element.54), channel_id=1, source_target_pairs={{0,64},{16,80},{32,96},{48,112},{64,0},{80,16},{96,32},{112,48},{1... | collective-permute-start | bytes 786440 | tf_op jit(solution)/shard_map/ppermute | solution.py:42
  53.8 9.9 %collective-permute-start.12 = (f32[512,128]{1,0:T(8,128)S(1)}, f32[512,128]{1,0:T(8,128)S(1)}, u32[]{:S(2)}, u32[]{:S(2)}) collective-permute-start(f32[512,128]{1,0:T(8,128)S(1)} %get-tuple-element.55), channel_id=1, source_target_pairs={{0,192},{16,208},{32,224},{48,240},{64,128},{80,144},{96,160},{112... | collective-permute-start | bytes 786440 | tf_op jit(solution)/shard_map/ppermute | solution.py:42
  55.1 8.5 %collective-permute-start.13 = (f32[256,128]{1,0:T(8,128)S(1)}, f32[256,128]{1,0:T(8,128)S(1)}, u32[]{:S(2)}, u32[]{:S(2)}) collective-permute-start(f32[256,128]{1,0:T(8,128)S(1)} %get-tuple-element.56), channel_id=1, source_target_pairs={{0,128},{16,144},{32,160},{48,176},{64,192},{80,208},{96,224},{112... | collective-permute-start | bytes 393224 | tf_op jit(solution)/shard_map/ppermute | solution.py:42
